TPU v7x, 128 devices: a whole 4x4x4 slice. The times are simulated.
128 devices in a mesh: section: 8 (over y, core), dev: 16 (over z, x).
Axes of the slice: x: 4, y: 4, z: 4, core: 2. Of those that a mesh axis runs over, the one named last changes fastest.
Arguments:
- activations: bfloat16 [8, 512, 8192], P('section', None, 'dev'), may hold values from -6 to 6
- q_weight: bfloat16 [8, 8192, 4096], P('section', None, 'dev'), may hold values from -0.125 to 0.125
- out_weight: bfloat16 [8, 4096, 8192], P('section', 'dev'), may hold values from -1 to 1
- kv_weight: bfloat16 [8, 8192, 2048], P('section', 'dev'), may hold values from -0.0625 to 0.0625
- passage_store: bfloat16 [8, 64, 8, 512, 256], P('section', 'dev'), may hold values from -400 to 400
- passage_home: int32 [8, 64], P('section'), may hold values from 0 to 63, as said below
- retrieved: int32 [8, 2, 8], P('section'), may hold values from 0 to 63, as said below
- slot_order: int32 [8, 2, 8], P('section'), may hold values from 0 to 7, each once within a row
- recomputed: int32 [8, 16, 77], P('section'), may hold values from 0 to 511, as said below
- passage_hidden: bfloat16 [8, 16, 77, 8192], P('section', None, None, 'dev'), may hold values from -6 to 6
Outputs:
- passed_on: bfloat16 [8, 512, 8192], P('section', None, 'dev')
Inputs may be any that keep to these rules, and one draw needn't show every extreme that they name: `passage_home`: for each section a permutation; rows r * 4 to (r + 1) * 4 - 1 of a section's store lie on device r of dev. The 8 passages of one request differ. In each section, at most 2 of the 16 retrieved entries name passages stored on one device, and some device has exactly 2. `recomputed`: increasing within each slot.
All inputs are finite; a program needn't handle non-finite values.
Results may differ from a plain program's by a relative error of at most 0.035.
The roundings to bfloat16 on the way count: a program that leaves them out, or rounds other values in their place, can miss the bound.
Values may be sent and summed in bfloat16 or wider, within the bound.
A program may use at most 192 MiB of HBM per device.

v0:
```python
import jax
import jax.numpy as jnp
from jax import lax
from jax.sharding import PartitionSpec as P

QH = 32
KVH = 8
HD = 128
PASS_LEN = 512
TOPK = 8
RECOMP = 77
REQ_SECTION = 2
QLEN = 256
SLOTS = 16


ROPE_BASE = 500000.0


def partner_2(block, axis, bit):
    count = lax.axis_size(axis)
    route = []
    for low in range(count):
        high = low | 1 << bit
        if high != low and high < count:
            route += [(low, high), (high, low)]
    return lax.ppermute(block, axis, route)


def from_behind(value, axis, steps):
    count = lax.axis_size(axis)
    pairs = [(source, (source + steps) % count) for source in range(count)]
    return lax.ppermute(value, axis, pairs)


def rotate(vectors, positions):
    half_dim = HD // 2
    frequency = ROPE_BASE ** (-(jnp.arange(half_dim, dtype=jnp.float32) * (2.0 / HD)))
    angles = positions.astype(jnp.float32)[..., None] * frequency
    cosine = jnp.cos(angles)
    sine_part = jnp.sin(angles)
    first_half = vectors[..., :half_dim]
    second_half = vectors[..., half_dim:]
    return jnp.concatenate(
        [
            first_half * cosine - second_half * sine_part,
            second_half * cosine + first_half * sine_part,
        ],
        axis=-1,
    )


def blend_slot(block_kv, places, fresh_rows):
    return block_kv.at[places].set(fresh_rows)


def body(
    activations,
    q_weight,
    out_weight,
    kv_weight,
    passage_store,
    passage_home,
    retrieved,
    slot_order,
    recomputed,
    passage_hidden,
):
    inputs = activations[0]
    query_rows = inputs.shape[0]
    devices = lax.axis_size("dev")
    rank_here = lax.axis_index("dev")
    query_proj = q_weight[0]
    heads_here = query_proj.shape[1] // HD
    group_size = QH // KVH
    token_pos = TOPK * PASS_LEN + jnp.arange(QLEN, dtype=jnp.int32)
    queries = jnp.dot(
        lax.all_gather(inputs, "dev", axis=1, tiled=True),
        query_proj,
        preferred_element_type=jnp.float32,
    )
    queries = rotate(
        queries.reshape(REQ_SECTION, QLEN, heads_here, HD), token_pos[None, :, None]
    ).astype(jnp.bfloat16)
    local_rows = jnp.concatenate([inputs, passage_hidden[0].reshape(-1, inputs.shape[1])], axis=0)
    partial_kv = jnp.dot(local_rows, kv_weight[0], preferred_element_type=jnp.float32)
    dest_heads = jnp.arange(devices, dtype=jnp.int32) * heads_here // group_size
    own_part = lax.psum_scatter(
        partial_kv.astype(jnp.bfloat16), "dev", scatter_dimension=1, tiled=True
    )
    partner = partner_2(own_part, "dev", 0)
    keys_values = jnp.where(
        rank_here % 2 == 0,
        jnp.concatenate([own_part, partner], axis=1),
        jnp.concatenate([partner, own_part], axis=1),
    )
    own_rows = keys_values[:query_rows].reshape(REQ_SECTION, QLEN, 2 * HD)
    own_keys = rotate(own_rows[..., :HD].astype(jnp.float32), token_pos[None, :]).astype(
        jnp.bfloat16
    )
    own_values = own_rows[..., HD:]
    fresh_rows = keys_values[query_rows:].reshape(SLOTS, RECOMP, 2 * HD)
    recomp_all = recomputed[0]
    offsets = slot_order[0].reshape(SLOTS) * PASS_LEN
    fresh_keys = rotate(
        fresh_rows[..., :HD].astype(jnp.float32), offsets[:, None] + recomp_all
    ).astype(jnp.bfloat16)
    fresh_rows = jnp.concatenate([fresh_keys, fresh_rows[..., HD:]], axis=-1)
    store_here = passage_store[0]
    per_device = store_here.shape[0]
    home_rows = passage_home[0][retrieved[0].reshape(SLOTS)]
    owners = home_rows // per_device
    store_slot = home_rows % per_device
    outgoing = store_here[:, dest_heads]
    arrived = lax.all_to_all(outgoing, "dev", split_axis=1, concat_axis=1, tiled=True)
    fetched = arrived[store_slot, owners]
    moved_keys = rotate(fetched[..., :HD].astype(jnp.float32), offsets[:, None]).astype(
        jnp.bfloat16
    )
    fetched = jnp.concatenate([moved_keys, fetched[..., HD:]], axis=-1)
    blended = jax.vmap(blend_slot)(fetched, recomp_all, fresh_rows)
    context = blended.reshape(REQ_SECTION, TOPK * PASS_LEN, 2 * HD)
    score_scale = HD ** (-0.5)
    far_scores = (
        jnp.einsum("rqhd,rkd->rhqk", queries, context[..., :HD], preferred_element_type=jnp.float32)
        * score_scale
    )
    near_scores = (
        jnp.einsum("rqhd,rkd->rhqk", queries, own_keys, preferred_element_type=jnp.float32)
        * score_scale
    )
    causal = jnp.arange(QLEN)[:, None] >= jnp.arange(QLEN)[None, :]
    near_scores = jnp.where(causal, near_scores, -jnp.inf)
    row_max = jnp.maximum(far_scores.max(axis=-1), near_scores.max(axis=-1))[..., None]
    far_exp = jnp.exp(far_scores - row_max)
    near_exp = jnp.exp(near_scores - row_max)
    denominator = far_exp.sum(axis=-1, keepdims=True) + near_exp.sum(axis=-1, keepdims=True)
    far_weights = (far_exp / denominator).astype(jnp.bfloat16)
    near_weights = (near_exp / denominator).astype(jnp.bfloat16)
    mixed_out = jnp.einsum(
        "rhqk,rkd->rqhd", far_weights, context[..., HD:], preferred_element_type=jnp.float32
    )
    mixed_out = mixed_out + jnp.einsum(
        "rhqk,rkd->rqhd", near_weights, own_values, preferred_element_type=jnp.float32
    )
    attended = mixed_out.astype(jnp.bfloat16).reshape(query_rows, heads_here * HD)
    partial_out = jnp.dot(attended, out_weight[0], preferred_element_type=jnp.float32)
    branch = lax.psum_scatter(
        partial_out.astype(jnp.bfloat16), "dev", scatter_dimension=1, tiled=True
    )
    passed = from_behind(branch, "section", 1)
    return passed[None]


def solution(mesh):
    in_specs = (
        P("section", None, "dev"),
        P("section", None, "dev"),
        P("section", "dev", None),
        P("section", "dev", None),
        P("section", "dev", None, None, None),
        P("section", None),
        P("section", None, None),
        P("section", None, None),
        P("section", None, None),
        P("section", None, None, "dev"),
    )
    out_specs = P("section", None, "dev")
    return jax.shard_map(body, mesh=mesh, in_specs=in_specs, out_specs=out_specs, check_vma=False)
```

profile of v0, /device:TPU:15, one launch (start us, length us, event | category | flops | bytes accessed | tf_op | source)
XLA Modules:
  0.0 583.2 jit_solution(7092717238945452684)
XLA Ops:
  6.5 2.1 copy.31
  8.7 1.3 reshape_squeeze.8
  10.0 7.3 %convolution_convert_fusion.1 = bf16[1744,2048]{1,0:T(8,128)(2,1)} fusion(bf16[1,512,2048]{2,1,0:T(8,128)(2,1)S(1)} %copy-done, bf16[1232,512]{1,0:T(8,128)(2,1)} %reshape_squeeze.8, bf16[512,512]{1,0:T(8,128)(2,1)} %bitcast.125), kind=kOutput, calls=%fused_computation.11 | convolution fusion | flops 3664576512 | bytes 11026432 | tf_op jit(solution)/shard_map/dot_general | solution.py:86
  17.3 10.1 %copy.56 = bf16[1744,2048]{0,1:T(8,128)(2,1)} copy(bf16[1744,2048]{1,0:T(8,128)(2,1)} %convolution_convert_fusion.1) | data formatting | bytes 14286848
  27.5 10.7 %gather_fusion = bf16[16,4,512,256]{3,2,1,0:T(8,128)(2,1)} fusion(bf16[4,8,512,256]{3,2,1,0:T(8,128)(2,1)} %bitcast.115, s32[1024]{0:T(1024)S(1)} %pad_clamp_fusion.1), kind=kCustom, calls=%fused_computation | custom fusion | bytes 33554496 | tf_op jit(solution)/shard_map/gather | solution.py:114
  38.1 7.8 %all-to-all-start = ((bf16[4,16,512,256]{3,2,0,1:T(8,128)(2,1)}), bf16[4,16,512,256]{3,2,0,1:T(8,128)(2,1)}, u32[]{:S(2)}, u32[]{:S(2)}) async-start(bf16[4,16,512,256]{3,2,0,1:T(8,128)(2,1)} %bitcast.114), calls=%async_computation | async-start | bytes 33554432 | tf_op jit(solution)/shard_map/all_to_all | solution.py:115
  46.0 0.7 all-gather.3.cloned.1.call-update
  47.3 6.4 %copy.53 = bf16[256,8192]{1,0:T(8,128)(2,1)} copy(bf16[256,8192]{0,1:T(8,128)(2,1)} %bitcast.120) | data formatting | bytes 8388608 | tf_op jit(solution)/shard_map/dot_general | solution.py:77
  54.2 0.7 gather_fusion.1
  54.9 0.7 iota_compare_fusion
  55.6 285.0 %reduce-scatter.7.cloned.1.call-done = bf16[128,1744]{1,0:T(8,128)(2,1)} async-done(((bf16[2048,1744]{1,0:T(8,128)(2,1)}), bf16[128,1744]{1,0:T(8,128)(2,1)}) %reduce-scatter.7.cloned.1.call-update) | async-done | bytes 446480
  340.6 1.3 copy.57
  341.9 0.5 collective-permute-start
  342.5 9.2 %collective-permute-done = bf16[1744,128]{1,0:T(8,128)(2,1)S(1)} collective-permute-done((bf16[1744,128]{1,0:T(8,128)(2,1)S(1)}, bf16[1744,128]{1,0:T(8,128)(2,1)S(1)}, u32[]{:S(2)}, u32[]{:S(2)}) %collective-permute-start) | collective-permute-done | bytes 446496 | tf_op jit(solution)/shard_map/ppermute | solution.py:27
  352.5 3.0 fusion.20
  356.0 0.8 subtract_convert_fusion.1
  356.8 8.6 %gather_fusion.2 = bf16[16,512,256]{2,1,0:T(8,128)(2,1)} fusion(bf16[4,16,512,256]{3,2,0,1:T(8,128)(2,1)} %all-to-all-done, s32[16]{0:T(128)S(1)} %fusion.36), kind=kCustom, calls=%fused_computation.2 | custom fusion | bytes 8388736 | tf_op jit(solution)/shard_map/gather | solution.py:116
  365.4 4.8 slice_convert_fusion
  370.2 50.9 %all-gather.3.cloned.1.call-done = bf16[1,512,8192]{2,1,0:T(8,128)(2,1)} async-done(((bf16[1,512,512]{2,1,0:T(8,128)(2,1)}), bf16[1,512,8192]{2,1,0:T(8,128)(2,1)}) %all-gather.3.cloned.1.call-update) | async-done | bytes 8388624 | tf_op jit(solution)/shard_map/all_gather | solution.py:78
  421.1 7.1 %fusion.42 = f32[2,256,2,128]{1,3,2,0:T(8,128)S(1)} fusion(bf16[2,256,8192,1]{2,1,3,0:T(8,128)(2,1)} %bitcast.128, bf16[2,128,8192,1]{2,1,0,3:T(8,128)(2,1)} %bitcast.121), kind=kOutput, calls=%fused_computation.103 | convolution fusion | flops 2147483648 | bytes 13107200 | tf_op jit(solution)/shard_map/dot_general | solution.py:77
  428.3 1.5 subtract_convert_fusion
  429.8 3.2 pad_maximum_fusion
  433.0 13.2 %scatter_fusion = bf16[8192,256]{1,0:T(8,128)(2,1)} fusion(bf16[8192,256]{1,0:T(8,128)(2,1)} %bitcast.116, s32[1232]{0:T(1024)S(1)} %reshape.496, bf16[1232,256]{1,0:T(8,128)(2,1)S(1)} %reshape.498), kind=kCustom, calls=%fused_computation.3 | custom fusion | bytes 1897280
  446.3 8.8 %bitcast_reduce_fusion = (f32[2,2,256]{2,1,0:T(2,128)S(1)}, f32[2,4096,256,2]{2,1,3,0:T(8,128)}) fusion(bf16[2,256,2,64]{1,3,2,0:T(8,128)(2,1)S(1)} %get-tuple-element.14, bf16[2,256,2,64]{1,3,2,0:T(8,128)(2,1)S(1)} %get-tuple-element.13, bf16[2,4096,256]{2,1,0:T(8,128)(2,1)} %bitcast.117), kind=kOutput, calls=%fused_computation.5 | convolution fusion | flops 1082653696 | bytes 19140608 | tf_op jit(solution)/shard_map/rqhd,rkd->rhqk/dot_general | solution.py:125
  455.6 8.5 %fusion.1 = f32[2,2,256]{2,1,0:T(2,128)S(1)} fusion(f32[2,4096,256,2]{2,1,3,0:T(8,128)} %get-tuple-element.22, f32[2,2,256]{2,1,0:T(2,128)S(1)} %max.7), kind=kLoop, calls=%fused_computation.8 | loop fusion | flops 12581888 | bytes 16785408 | tf_op jit(solution)/shard_map/reduce_sum | solution.py:137
  464.4 1.8 copy-done.4
  466.2 7.7 %fusion.13 = bf16[2,256,2,128]{1,3,2,0:T(8,128)(2,1)S(1)} fusion(f32[2,128,2,256]{3,1,2,0:T(8,128)S(1)} %fusion.23, f32[2,4096,256,2]{2,1,3,0:T(8,128)} %get-tuple-element.22, f32[2,2,256]{2,1,0:T(2,128)S(1)} %add.172, f32[2,2,256]{2,1,0:T(2,128)S(1)} %max.7, bf16[2,4096,256]{2,1,0:T(8,128)(2,1)S(1)} %bitcast.118), kind=kOutput, calls=%fused_computation.29 | convolution fusion | flops 1090781184 | bytes 19668992 | tf_op jit(solution)/shard_map/rhqk,rkd->rqhd/dot_general | solution.py:140
  474.1 7.8 %convolution_convert_fusion = bf16[512,8192]{1,0:T(8,128)(2,1)} fusion(bf16[1,256,8192]{2,1,0:T(8,128)(2,1)} %param.12, bf16[64,8,2,128]{3,2,1,0:T(2,128)(2,1)S(1)} %bitcast.122), kind=kOutput, calls=%fused_computation.9 | convolution fusion | flops 2151677952 | bytes 12845056 | tf_op jit(solution)/shard_map/dot_general | solution.py:147
  481.9 84.4 %reduce-scatter.5.cloned.1.call-done = bf16[512,512]{1,0:T(8,128)(2,1)} async-done(((bf16[512,8192]{1,0:T(8,128)(2,1)}), bf16[512,512]{1,0:T(8,128)(2,1)}) %reduce-scatter.5.cloned.1.call-update) | async-done | bytes 524304 | tf_op jit(solution)/shard_map/reduce_scatter | solution.py:148
  566.2 3.2 collective-permute-start.1
  569.4 6.4 %collective-permute-done.1 = bf16[512,512]{1,0:T(8,128)(2,1)S(1)} collective-permute-done((bf16[512,512]{1,0:T(8,128)(2,1)}, bf16[512,512]{1,0:T(8,128)(2,1)S(1)}, u32[]{:S(2)}, u32[]{:S(2)}) %collective-permute-start.1) | collective-permute-done | bytes 524320 | tf_op jit(solution)/shard_map/ppermute | solution.py:33
  575.9 0.8 copy.65
  (66 shorter events, 3.6 us)
Async XLA Ops:
  6.5 3.5 copy-start
  6.5 334.0 %reduce-scatter.7.cloned.1.call-start = ((), (), s32[]{:S(2)}) async-start(), calls=%async_computation.5 | async-start | bytes 7798784
  38.1 8.7 %copy-start.8 = (s32[1,2,8]{2,1,0:T(2,128)S(1)}, s32[1,2,8]{2,1,0:T(2,128)}, u32[]{:S(2)}) copy-start(s32[1,2,8]{2,1,0:T(2,128)} %param.17) | copy-start | bytes 196
  38.1 8.8 %copy-start.11 = (s32[1,2,8]{2,1,0:T(2,128)S(1)}, s32[1,2,8]{2,1,0:T(2,128)}, u32[]{:S(2)}) copy-start(s32[1,2,8]{2,1,0:T(2,128)} %param.16) | copy-start | bytes 196
  38.1 8.9 %copy-start.7 = (s32[1,16,77]{2,1,0:T(8,128)S(1)}, s32[1,16,77]{2,1,0:T(8,128)}, u32[]{:S(2)}) copy-start(s32[1,16,77]{2,1,0:T(8,128)} %param.18) | copy-start | bytes 14788
  38.1 8.9 %copy-start.10 = (s32[2]{0:T(128)S(1)}, s32[2]{0:T(128)}, u32[]{:S(2)}) copy-start(s32[2]{0:T(128)} %constant.86) | copy-start | bytes 28
  38.1 9.0 %copy-start.9 = (s32[2]{0:T(128)S(1)}, s32[2]{0:T(128)}, u32[]{:S(2)}) copy-start(s32[2]{0:T(128)} %constant.89) | copy-start | bytes 28
  38.1 318.7 %all-to-all-start = ((bf16[4,16,512,256]{3,2,0,1:T(8,128)(2,1)}), bf16[4,16,512,256]{3,2,0,1:T(8,128)(2,1)}, u32[]{:S(2)}, u32[]{:S(2)}) async-start(bf16[4,16,512,256]{3,2,0,1:T(8,128)(2,1)} %bitcast.114), calls=%async_computation | async-start | bytes 33554432 | tf_op jit(solution)/shard_map/all_to_all | solution.py:115
  46.0 375.1 %all-gather.3.cloned.1.call-start = ((), (), s32[]{:S(2)}) async-start(), calls=%async_computation.4 | async-start | bytes 8912896 | tf_op jit(solution)/shard_map/all_gather | solution.py:78
  46.7 519.5 %reduce-scatter.5.cloned.1.call-start = ((), (), s32[]{:S(2)}) async-start(), calls=%async_computation.3 | async-start | bytes 8912896 | tf_op jit(solution)/shard_map/reduce_scatter | solution.py:148
  47.3 6.9 %copy-start.2 = (s32[1,64]{1,0:T(1,128)S(1)}, s32[1,64]{1,0:T(1,128)}, u32[]{:S(2)}) copy-start(s32[1,64]{1,0:T(1,128)} %param.15) | copy-start | bytes 772
  341.9 9.9 %collective-permute-start = (bf16[1744,128]{1,0:T(8,128)(2,1)S(1)}, bf16[1744,128]{1,0:T(8,128)(2,1)S(1)}, u32[]{:S(2)}, u32[]{:S(2)}) collective-permute-start(bf16[1744,128]{1,0:T(8,128)(2,1)S(1)} %copy.57), channel_id=1, source_target_pairs={{0,1},{1,0},{2,3},{3,2},{4,5},{5,4},{6,7},{7,6},{8,9},{9,8},{10,11... | collective-permute-start | bytes 1339400 | tf_op jit(solution)/shard_map/ppermute | solution.py:27
  421.1 7.2 %copy-start.3 = (f32[16,512,128]{2,1,0:T(8,128)S(1)}, f32[16,512,128]{2,1,0:T(8,128)}, u32[]{:S(2)}) copy-start(f32[16,512,128]{2,1,0:T(8,128)} %get-tuple-element.7) | copy-start | bytes 12582916
  446.3 8.8 %copy-start.5 = (bf16[2,256,64]{2,1,0:T(8,128)(2,1)S(1)}, bf16[2,256,64]{2,1,0:T(8,128)(2,1)}, u32[]{:S(2)}) copy-start(bf16[2,256,64]{2,1,0:T(8,128)(2,1)} %get-tuple-element.16) | copy-start | bytes 196612
  446.3 8.8 %copy-start.6 = (pred[256,256]{0,1:T(8,128)(4,1)S(1)}, pred[256,256]{0,1:T(8,128)(4,1)}, u32[]{:S(2)}) copy-start(pred[256,256]{0,1:T(8,128)(4,1)} %iota_compare_fusion) | copy-start | bytes 196612
  464.1 2.2 copy-start.4
  481.9 94.8 %copy-start.1 = (bf16[1,512,2048]{2,1,0:T(8,128)(2,1)S(1)}, bf16[1,512,2048]{2,1,0:T(8,128)(2,1)}, u32[]{:S(2)}) copy-start(bf16[1,512,2048]{2,1,0:T(8,128)(2,1)} %param.13) | copy-start | bytes 6291460
  566.2 9.6 %collective-permute-start.1 = (bf16[512,512]{1,0:T(8,128)(2,1)}, bf16[512,512]{1,0:T(8,128)(2,1)S(1)}, u32[]{:S(2)}, u32[]{:S(2)}) collective-permute-start(bf16[512,512]{1,0:T(8,128)(2,1)} %reduce-scatter.5.cloned.1.call-done), channel_id=1, source_target_pairs={{0,16},{16,32},{32,48},{48,64},{64,80},{80,96},{96,112},{112,0},{1... | collective-permute-start | bytes 1572872 | tf_op jit(solution)/shard_map/ppermute | solution.py:33
Sparse Core Ops, SparseCore 0:
  27.5 312.9 reduce-scatter.6
  342.9 78.1 all-gather.2
  482.0 84.1 reduce-scatter.4
where the time goes:
time: 586 us; the launch traced here: 583 us
  waiting for transfers between devices  437 us (75%)
  local copies, waits for them, and re-layouts  58.1 us (10%)
  matrix products  39.3 us (7%)
  other arithmetic  24.1 us (4%)
  between operations  13.4 us (2%)
  starting transfers between devices  11.7 us (2%)
    unnamed x4, waiting for transfers between devices  286 us
    reduce_scatter x1, waiting for transfers between devices, body(): lax.psum_scatter(partial_out.astype(jnp.bfloat16), 'dev', scatter_dimensi...  84.4 us
    all_gather x1, waiting for transfers between devices, body(): lax.all_gather(inputs, 'dev', axis=1, tiled=True)  50.9 us
    unnamed x31, local copies, waits for them, and re-layouts  29.5 us
  transfers between devices with their start and end apart: 6, of which 5 were waited for; matrix products, arithmetic and copies ran while one was open for 7% of the time, Pallas kernels for 0%

commit v1 on v0

v1 whole, which is shorter than its diff:
```python
import functools

import jax
import jax.numpy as jnp
from jax import lax
from jax.experimental import pallas as pl
from jax.experimental.pallas import tpu as pltpu
from jax.sharding import PartitionSpec as P

QH = 32
KVH = 8
HD = 128
PASS_LEN = 512
TOPK = 8
RECOMP = 77
REQ_SECTION = 2
QLEN = 256
SLOTS = 16
CAP = 2
SIDE = 4
N_DEV = 16
PAD = 80
GROUP = QLEN + TOPK * PAD
KEPT = PASS_LEN - RECOMP
HALF = 224
ROPE_BASE = 500000.0
MESH = pl.DeviceIdType.MESH
F32 = jnp.float32
BF16 = jnp.bfloat16
SCALE = HD**-0.5 * 1.4426950408889634


def tables(positions):
    half_dim = HD // 2
    frequency = ROPE_BASE ** (-(jnp.arange(half_dim, dtype=F32) * (2.0 / HD)))
    angles = positions.astype(F32)[..., None] * frequency
    cosine, sine = jnp.cos(angles), jnp.sin(angles)
    return (
        jnp.concatenate([cosine, cosine], axis=-1),
        jnp.concatenate([-sine, sine], axis=-1),
    )


def turned(v, cosine, sine):
    return v * cosine + pltpu.roll(v, HD // 2, axis=1) * sine


def place():
    d = lax.axis_index("dev")
    return lax.axis_index("section"), d // SIDE, lax.rem(d, SIDE)


def around(v, step):
    return lax.rem(v + step + SIDE, SIDE)


def remote(src, dst, send, recv, target):
    return pltpu.make_async_remote_copy(
        src_ref=src,
        dst_ref=dst,
        send_sem=send,
        recv_sem=recv,
        device_id=target,
        device_id_type=MESH,
    )


def pack_kernel(rows, store, keep, cosine, sine, out):
    lanes = lax.broadcasted_iota(jnp.int32, (2 * HALF, PASS_LEN), 1)
    pick = (lanes == keep[0]).astype(F32).astype(BF16)
    for h in range(4):
        kept = jnp.dot(pick, store[0, h], preferred_element_type=F32)
        keys = turned(kept[:, :HD], cosine[0], sine[0]).astype(BF16)
        values = kept[:, HD:].astype(BF16)
        for half in range(2):
            span = slice(half * HALF, (half + 1) * HALF)
            out[h, half, 0, :, :HD] = keys[span]
            out[h, half, 0, :, HD:] = values[span]


def pack(rows, store, keep, cosine, sine):
    out = pl.pallas_call(
        pack_kernel,
        out_shape=jax.ShapeDtypeStruct((KVH, 2, CAP, HALF, 2 * HD), BF16),
        grid_spec=pltpu.PrefetchScalarGridSpec(
            num_scalar_prefetch=1,
            grid=(CAP, 2),
            in_specs=[
                pl.BlockSpec((1, 4, PASS_LEN, 2 * HD), lambda c, g, rows: (rows[c], g, 0, 0)),
                pl.BlockSpec((1, 2 * HALF, 1), lambda c, g, rows: (c, 0, 0)),
                pl.BlockSpec((1, 1, HD), lambda c, g, rows: (c, 0, 0)),
                pl.BlockSpec((1, 1, HD), lambda c, g, rows: (c, 0, 0)),
            ],
            out_specs=pl.BlockSpec(
                (4, 2, 1, HALF, 2 * HD), lambda c, g, rows: (g, 0, c, 0, 0)
            ),
        ),
        compiler_params=pltpu.CompilerParams(vmem_limit_bytes=40 * 2**20),
        name="pack",
    )(rows, store, keep, cosine, sine)
    return out.reshape(N_DEV, CAP, HALF, 2 * HD)


def front_kernel(
    x, hid, kvw, qw, sent, cosq, sinq,
    q_out, kv_out, st_out,
    xall, qv, kvv, hidv, rows, pa, pb, l1, r1, l2, r2, z2, qacc,
    loc, ag_s, ag_r, rs_s, rs_r, st_s, st_r, q_s, q_r,
):
    sec, z, x_ = place()
    me = z * SIDE + x_

    def at(zz, xx):
        return (sec, zz * SIDE + xx)

    right, left = at(z, around(x_, 1)), at(z, around(x_, -1))
    down, up = at(around(z, 1), x_), at(around(z, -1), x_)
    pair = (sec, me + 1 - 2 * lax.rem(me, 2))

    barrier = pltpu.get_barrier_semaphore()
    for k in range(1, N_DEV):
        pl.semaphore_signal(
            barrier, inc=1, device_id=(sec, lax.rem(me + k, N_DEV)), device_id_type=MESH
        )
    loads = [
        pltpu.make_async_copy(kvw, kvv, loc.at[0]),
        pltpu.make_async_copy(hid, hidv, loc.at[1]),
        pltpu.make_async_copy(x.at[pl.ds(0, QLEN)], rows.at[0, pl.ds(0, QLEN)], loc.at[2]),
        pltpu.make_async_copy(x.at[pl.ds(QLEN, QLEN)], rows.at[1, pl.ds(0, QLEN)], loc.at[3]),
        pltpu.make_async_copy(x.at[pl.ds(0, QLEN)], xall.at[0, me], loc.at[4]),
        pltpu.make_async_copy(x.at[pl.ds(QLEN, QLEN)], xall.at[1, me], loc.at[5]),
        pltpu.make_async_copy(qw, qv, loc.at[6]),
        pltpu.make_async_copy(sent.at[me], st_out.at[me], loc.at[7]),
    ]
    for load in loads:
        load.start()
    pl.semaphore_wait(barrier, N_DEV - 1)

    def chunk(half, first, second):
        if half == 0:
            return around(z, second) * SIDE + around(x_, first)
        return around(z, first) * SIDE + around(x_, second)

    ahead = [(right, left), (down, up)]
    top, bottom = pl.ds(0, QLEN // 2), pl.ds(QLEN // 2, QLEN // 2)
    whole = pl.ds(0, QLEN)
    sends = []

    def ag(half, src, span, sem, target, own=False):
        to = xall.at[half, src, span]
        frm = x.at[pl.ds(half * QLEN, QLEN)] if own else to
        copy = remote(frm, to, ag_s.at[sem], ag_r.at[sem], target)
        copy.start()
        sends.append(copy)

    def ag_wait(half, src, span, sem):
        to = xall.at[half, src, span]
        remote(to, to, ag_s.at[sem], ag_r.at[sem], right).wait_recv()

    for half in range(2):
        ag(half, me, whole, 20 * half, ahead[half][0], True)
        ag(half, me, whole, 20 * half + 1, ahead[half][1], True)
    for half in range(2):
        ag(half, me, whole, 20 * half + 4, ahead[1 - half][0], True)
        ag(half, me, whole, 20 * half + 5, ahead[1 - half][1], True)

    for k in (0, 1, 2, 3):
        loads[k].wait()
    for j in range(SLOTS):
        block = rows.at[j // TOPK, pl.ds(QLEN + (j % TOPK) * PAD, PAD)]
        block[...] = jnp.zeros_like(block)
        block[pl.ds(0, RECOMP)] = hidv[j]

    def project(k, carry):
        xx = around(x_, 2 + k // SIDE)
        zz = around(z, 2 + lax.rem(k, SIDE))
        head = 2 * zz + xx // 2
        span = pl.ds(pl.multiple_of(head * 2 * HD, 2 * HD), 2 * HD)
        part = jnp.dot(rows[lax.rem(xx, 2)], kvv[:, span], preferred_element_type=F32)
        part = part.astype(BF16)
        pa[xx, zz] = part[:, :HD]
        pb[zz, xx] = part[:, HD:]
        return carry

    lax.fori_loop(0, N_DEV, project, 0)

    parts = [pa, pb]
    spot = [x_, z]

    def rs(half, src, dst, sem, target):
        copy = remote(src, dst, rs_s.at[sem], rs_r.at[sem], target)
        copy.start()
        sends.append(copy)

    lo, hi = pl.ds(0, 2), pl.ds(2, 2)
    for half in range(2):
        p, c, b = parts[half], spot[half], 9 * half
        rs(half, p.at[around(c, 2), lo], l1.at[half], b, ahead[half][0])
        rs(half, p.at[around(c, 2), hi], r1.at[half], b + 1, ahead[half][1])
        rs(half, p.at[around(c, 1), hi], l2.at[half, hi], b + 2, ahead[half][0])
        rs(half, p.at[around(c, -1), lo], r2.at[half, lo], b + 3, ahead[half][1])

    for half in range(2):
        b = 20 * half
        src = chunk(half, -1, 0)
        ag_wait(half, src, whole, b)
        ag(half, src, top, b + 2, ahead[half][0])
        ag(half, src, whole, b + 8, ahead[1 - half][0])
        ag(half, src, whole, b + 9, ahead[1 - half][1])
        src = chunk(half, 1, 0)
        ag_wait(half, src, whole, b + 1)
        ag(half, src, bottom, b + 3, ahead[half][1])
        ag(half, src, whole, b + 12, ahead[1 - half][0])
        ag(half, src, whole, b + 13, ahead[1 - half][1])
    for half in range(2):
        b = 20 * half
        src = chunk(half, 2, 0)
        ag_wait(half, src, top, b + 2)
        ag_wait(half, src, bottom, b + 3)
        ag(half, src, whole, b + 16, ahead[1 - half][0])
        ag(half, src, whole, b + 17, ahead[1 - half][1])

    def second_axis(k, first):
        for half in range(2):
            b = 20 * half + 4 + 4 * k
            src = chunk(half, first, -1)
            ag_wait(half, src, whole, b)
            ag(half, src, top, b + 2, ahead[1 - half][0])
            src = chunk(half, first, 1)
            ag_wait(half, src, whole, b + 1)
            ag(half, src, bottom, b + 3, ahead[1 - half][1])

    second_axis(0, 0)

    for half in range(2):
        p, c, b = parts[half], spot[half], 9 * half
        remote(l1.at[half], l1.at[half], rs_s.at[b], rs_r.at[b], right).wait_recv()
        for u in range(2):
            block = p.at[around(c, 1), u]
            block[...] = (block[...].astype(F32) + l1[half, u].astype(F32)).astype(BF16)
        rs(half, p.at[around(c, 1), lo], l2.at[half, lo], b + 4, ahead[half][0])
        remote(r1.at[half], r1.at[half], rs_s.at[b + 1], rs_r.at[b + 1], right).wait_recv()
        for u in range(2):
            block = p.at[around(c, -1), 2 + u]
            block[...] = (block[...].astype(F32) + r1[half, u].astype(F32)).astype(BF16)
        rs(half, p.at[around(c, -1), hi], r2.at[half, hi], b + 5, ahead[half][1])

    second_axis(1, -1)
    second_axis(2, 1)
    second_axis(3, 2)

    for k in range(1, N_DEV):
        other = lax.rem(me + k, N_DEV)
        copy = remote(sent.at[other], st_out.at[me], st_s.at[k], st_r.at[k], (sec, other))
        copy.start()
        sends.append(copy)

    for half in range(2):
        p, c, b = parts[half], spot[half], 9 * half
        remote(l2.at[half, hi], l2.at[half, hi], rs_s.at[b + 2], rs_r.at[b + 2], right).wait_recv()
        remote(r2.at[half, lo], r2.at[half, lo], rs_s.at[b + 3], rs_r.at[b + 3], right).wait_recv()
        remote(l2.at[half, lo], l2.at[half, lo], rs_s.at[b + 4], rs_r.at[b + 4], right).wait_recv()
        remote(r2.at[half, hi], r2.at[half, hi], rs_s.at[b + 5], rs_r.at[b + 5], right).wait_recv()
        for u in range(SIDE):
            block = p.at[c, u]
            total = block[...].astype(F32) + l2[half, u].astype(F32) + r2[half, u].astype(F32)
            block[...] = total.astype(BF16)
        for k in range(1, SIDE):
            other = around(spot[1 - half], k)
            target = at(other, x_) if half == 0 else at(z, other)
            rs(half, p.at[c, other], z2.at[half, k - 1], b + 5 + k, target)

    for k in (4, 5, 6):
        loads[k].wait()
    for half in range(2):
        for k in range(SIDE):
            b = 20 * half + 4 + 4 * k
            src = chunk(half, (0, -1, 1, 2)[k], 2)
            ag_wait(half, src, top, b + 2)
            ag_wait(half, src, bottom, b + 3)

    def project_queries(k, carry):
        span = pl.ds(pl.multiple_of(k * 2 * QLEN, 2 * QLEN), 2 * QLEN)
        weight = qv[span, :]
        for half in range(2):
            qacc[half] += jnp.dot(xall[half, k], weight, preferred_element_type=F32)
        return carry

    qacc[...] = jnp.zeros_like(qacc)
    lax.fori_loop(0, N_DEV, project_queries, 0)
    base = 2 * lax.rem(me, 2)
    for half in range(2):
        for j in range(2):
            head = turned(qacc[half, :, j * HD : (j + 1) * HD], cosq[...], sinq[...])
            q_out[half, base + j] = head.astype(BF16)
        block = q_out.at[half, pl.ds(base, 2)]
        copy = remote(block, block, q_s.at[half], q_r.at[half], pair)
        copy.start()
        sends.append(copy)

    for half in range(2):
        p, c, b = parts[half], spot[half], 9 * half
        total = p[c, spot[1 - half]].astype(F32)
        for k in range(1, SIDE):
            block = z2.at[half, k - 1]
            remote(block, block, rs_s.at[b + 5 + k], rs_r.at[b + 5 + k], right).wait_recv()
            total += block[...].astype(F32)
        kv_out[:, half * HD : (half + 1) * HD] = total.astype(BF16)

    for half in range(2):
        block = q_out.at[half, pl.ds(2 - base, 2)]
        remote(block, block, q_s.at[half], q_r.at[half], pair).wait_recv()
    loads[7].wait()
    for k in range(1, N_DEV):
        block = st_out.at[lax.rem(me + N_DEV - k, N_DEV)]
        remote(block, block, st_s.at[k], st_r.at[k], right).wait_recv()
    for copy in sends:
        copy.wait_send()


def front(x, hid, kvw, qw, sent, cosq, sinq):
    anywhere = pl.BlockSpec(memory_space=pl.ANY)
    vmem = pl.BlockSpec(memory_space=pltpu.VMEM)
    dma = pltpu.SemaphoreType.DMA
    d_here = x.shape[1]
    return pl.pallas_call(
        front_kernel,
        out_shape=(
            jax.ShapeDtypeStruct((REQ_SECTION, 4, QLEN, HD), BF16),
            jax.ShapeDtypeStruct((GROUP, 2 * HD), BF16),
            jax.ShapeDtypeStruct((N_DEV, CAP, HALF, 2 * HD), BF16),
        ),
        in_specs=[anywhere] * 5 + [vmem] * 2,
        out_specs=(vmem, vmem, anywhere),
        scratch_shapes=[
            pltpu.VMEM((2, N_DEV, QLEN, d_here), BF16),
            pltpu.VMEM(qw.shape, BF16),
            pltpu.VMEM(kvw.shape, BF16),
            pltpu.VMEM(hid.shape, BF16),
            pltpu.VMEM((REQ_SECTION, GROUP, d_here), BF16),
            pltpu.VMEM((SIDE, SIDE, GROUP, HD), BF16),
            pltpu.VMEM((SIDE, SIDE, GROUP, HD), BF16),
            pltpu.VMEM((2, 2, GROUP, HD), BF16),
            pltpu.VMEM((2, 2, GROUP, HD), BF16),
            pltpu.VMEM((2, SIDE, GROUP, HD), BF16),
            pltpu.VMEM((2, SIDE, GROUP, HD), BF16),
            pltpu.VMEM((2, SIDE - 1, GROUP, HD), BF16),
            pltpu.VMEM((2, QLEN, 2 * HD), F32),
            dma((8,)),
            dma((40,)),
            dma((40,)),
            dma((18,)),
            dma((18,)),
            dma((N_DEV,)),
            dma((N_DEV,)),
            dma((2,)),
            dma((2,)),
        ],
        compiler_params=pltpu.CompilerParams(
            collective_id=0, has_side_effects=True, vmem_limit_bytes=56 * 2**20
        ),
        name="front",
    )(x, hid, kvw, qw, sent, cosq, sinq)


def attend_kernel(entry, mine, q, kv, st, cosk, sink, bias, o, lse, acc, m, l, ks):
    p = mine[0]
    ks[...] = turned(kv[:, :HD].astype(F32), cosk[...], sink[...]).astype(BF16)
    cols = 4 * QLEN

    def step(scores, values):
        old = m[...]
        new = jnp.maximum(old, jnp.max(scores, axis=0, keepdims=True))
        weights = jnp.exp2(scores - new)
        scale = jnp.exp2(old - new)
        m[...] = new
        l[...] = l[...] * scale + jnp.sum(weights, axis=0, keepdims=True)
        acc[...] = acc[...] * scale + lax.dot_general(
            values, weights.astype(BF16), (((0,), (0,)), ((), ())), preferred_element_type=F32
        )

    def score(keys, queries):
        s = lax.dot_general(
            keys, queries, (((1,), (1,)), ((), ())), preferred_element_type=F32
        )
        return s * SCALE

    for r in range(REQ_SECTION):
        m[...] = jnp.full_like(m, -1e30)
        l[...] = jnp.zeros_like(l)
        acc[...] = jnp.zeros_like(acc)
        queries = q[r].reshape(cols, HD)
        for k in range(TOPK):
            e = entry[r * TOPK + k]
            block = st.at[e]
            s = score(block[:, :HD], queries) + bias[pl.ds(0, HALF)]
            step(s, block[:, HD:])

        @pl.when(p == r)
        def _():
            for k in range(TOPK // 2):
                span = pl.ds(QLEN + 2 * k * PAD, 2 * PAD)
                s = score(ks[span, :], queries) + bias[pl.ds(HALF, 2 * PAD)]
                step(s, kv[span, HD:])
            s = score(ks[pl.ds(0, QLEN), :], queries)
            keys_at = lax.broadcasted_iota(jnp.int32, (QLEN, cols), 0)
            query_at = lax.rem(lax.broadcasted_iota(jnp.int32, (QLEN, cols), 1), QLEN)
            s = jnp.where(keys_at <= query_at, s, -jnp.inf)
            step(s, kv[pl.ds(0, QLEN), HD:])

        done = (acc[...] / l[...]).astype(BF16)
        level = m[...] + jnp.log2(l[...])
        for j in range(4):
            span = slice(j * QLEN, (j + 1) * QLEN)
            here = pl.ds(r * QLEN, QLEN)
            o[j // 2, pl.ds((j % 2) * HD, HD), here] = done[:, span]
            lse[j // 2, pl.ds(j % 2, 1), here] = level[:, span]


def attend(entry, mine, q, kv, st, cosk, sink, bias):
    vmem = pl.BlockSpec(memory_space=pltpu.VMEM)
    smem = pl.BlockSpec(memory_space=pltpu.SMEM)
    return pl.pallas_call(
        attend_kernel,
        out_shape=(
            jax.ShapeDtypeStruct((2, 2 * HD, REQ_SECTION * QLEN), BF16),
            jax.ShapeDtypeStruct((2, 8, REQ_SECTION * QLEN), F32),
        ),
        in_specs=[smem, smem] + [vmem] * 6,
        out_specs=(vmem, vmem),
        scratch_shapes=[
            pltpu.VMEM((HD, 4 * QLEN), F32),
            pltpu.VMEM((1, 4 * QLEN), F32),
            pltpu.VMEM((1, 4 * QLEN), F32),
            pltpu.VMEM((GROUP, HD), BF16),
        ],
        compiler_params=pltpu.CompilerParams(vmem_limit_bytes=48 * 2**20),
        name="attend",
    )(entry, mine, q, kv, st, cosk, sink, bias)


BLOCKS = 2


def back_kernel(
    o, lse, ow, out,
    wv, other_o, other_lse, att, pa, pb, l1, r1, l2, r2, z2,
    loc, ex_s, ex_r, rs_s, rs_r,
):
    sec, z, x_ = place()
    me = z * SIDE + x_
    sections = lax.axis_size("section")
    after, before = lax.rem(sec + 1, sections), lax.rem(sec + sections - 1, sections)
    mine = lax.rem(me, 2)

    def at(zz, xx):
        return (sec, zz * SIDE + xx)

    right, left = at(z, around(x_, 1)), at(z, around(x_, -1))
    down, up = at(around(z, 1), x_), at(around(z, -1), x_)
    pair = (sec, me + 1 - 2 * mine)
    barrier = pltpu.get_barrier_semaphore()
    greeted = [right, left, down, up]
    for s in (after, before):
        greeted.append((s, me))
        for k in range(1, SIDE):
            greeted.append((s, z * SIDE + around(x_, k)))
            greeted.append((s, around(z, k) * SIDE + x_))
    for target in greeted:
        pl.semaphore_signal(barrier, inc=1, device_id=target, device_id_type=MESH)
    load = pltpu.make_async_copy(ow, wv, loc.at[0])
    load.start()
    pl.semaphore_wait(barrier, len(greeted))
    sends = []

    def push(src, dst, send, recv, target):
        copy = remote(src, dst, send, recv, target)
        copy.start()
        sends.append(copy)

    push(o.at[1 - mine], other_o, ex_s.at[0], ex_r.at[0], pair)
    push(lse.at[1 - mine], other_lse, ex_s.at[1], ex_r.at[1], pair)
    remote(other_o, other_o, ex_s.at[0], ex_r.at[0], pair).wait_recv()
    remote(other_lse, other_lse, ex_s.at[1], ex_r.at[1], pair).wait_recv()
    for j in range(2):
        a, b = lse[mine, pl.ds(j, 1), :], other_lse[pl.ds(j, 1), :]
        most = jnp.maximum(a, b)
        a, b = jnp.exp2(a - most), jnp.exp2(b - most)
        span = pl.ds(j * HD, HD)
        joined = o[mine, span, :].astype(F32) * a + other_o[span, :].astype(F32) * b
        joined = joined / (a + b)
        att[:, j * HD : (j + 1) * HD] = joined.T.astype(BF16)
    load.wait()

    ahead = [(right, left), (down, up)]
    spot = [x_, z]
    parts = [pa, pb]
    lo, hi = pl.ds(0, 2), pl.ds(2, 2)
    size = REQ_SECTION * QLEN // BLOCKS
    part = size // 2

    def compute(b):
        def one(k, carry):
            xx = around(x_, 2 + k // SIDE)
            zz = around(z, 2 + lax.rem(k, SIDE))
            span = pl.ds(pl.multiple_of((zz * SIDE + xx) * 512, 512), 512)
            got = jnp.dot(
                att[b * size : (b + 1) * size, :], wv[:, span], preferred_element_type=F32
            ).astype(BF16)
            pa[b, xx, zz] = got[:part]
            pb[b, zz, xx] = got[part:]
            return carry

        lax.fori_loop(0, N_DEV, one, 0)

    def first(b):
        for half in range(2):
            p, c, s = parts[half], spot[half], 20 * b + 10 * half
            push(p.at[b, around(c, 2), lo], l1.at[b, half], rs_s.at[s], rs_r.at[s], ahead[half][0])
            push(p.at[b, around(c, 2), hi], r1.at[b, half], rs_s.at[s + 1], rs_r.at[s + 1], ahead[half][1])
            push(p.at[b, around(c, 1), hi], l2.at[b, half, hi], rs_s.at[s + 2], rs_r.at[s + 2], ahead[half][0])
            push(p.at[b, around(c, -1), lo], r2.at[b, half, lo], rs_s.at[s + 3], rs_r.at[s + 3], ahead[half][1])

    def arrived(block, s):
        remote(block, block, rs_s.at[s], rs_r.at[s], right).wait_recv()

    def second(b):
        for half in range(2):
            p, c, s = parts[half], spot[half], 20 * b + 10 * half
            arrived(l1.at[b, half], s)
            for u in range(2):
                block = p.at[b, around(c, 1), u]
                block[...] = (block[...].astype(F32) + l1[b, half, u].astype(F32)).astype(BF16)
            push(p.at[b, around(c, 1), lo], l2.at[b, half, lo], rs_s.at[s + 4], rs_r.at[s + 4], ahead[half][0])
            arrived(r1.at[b, half], s + 1)
            for u in range(2):
                block = p.at[b, around(c, -1), 2 + u]
                block[...] = (block[...].astype(F32) + r1[b, half, u].astype(F32)).astype(BF16)
            push(p.at[b, around(c, -1), hi], r2.at[b, half, hi], rs_s.at[s + 5], rs_r.at[s + 5], ahead[half][1])

    def third(b):
        for half in range(2):
            p, c, s = parts[half], spot[half], 20 * b + 10 * half
            arrived(l2.at[b, half, hi], s + 2)
            arrived(r2.at[b, half, lo], s + 3)
            arrived(l2.at[b, half, lo], s + 4)
            arrived(r2.at[b, half, hi], s + 5)
            for u in range(SIDE):
                block = p.at[b, c, u]
                total = block[...].astype(F32) + l2[b, half, u].astype(F32)
                block[...] = (total + r2[b, half, u].astype(F32)).astype(BF16)
            for k in range(SIDE):
                other = around(spot[1 - half], k)
                target = (after, other * SIDE + x_) if half == 0 else (after, z * SIDE + other)
                push(p.at[b, c, other], z2.at[b, half, k], rs_s.at[s + 6 + k], rs_r.at[s + 6 + k], target)

    def fourth(b):
        for half in range(2):
            s = 20 * b + 10 * half
            total = None
            for k in range(SIDE):
                arrived(z2.at[b, half, k], s + 6 + k)
                block = z2[b, half, k].astype(F32)
                total = block if total is None else total + block
            out[pl.ds(b * size + half * part, part), :] = total.astype(BF16)

    compute(0)
    first(0)
    for b in range(BLOCKS):
        if b + 1 < BLOCKS:
            compute(b + 1)
            first(b + 1)
        second(b)
        if b > 0:
            third(b - 1)
    third(BLOCKS - 1)
    for b in range(BLOCKS):
        fourth(b)
    for copy in sends:
        copy.wait_send()


def back(o, lse, ow):
    vmem = pl.BlockSpec(memory_space=pltpu.VMEM)
    dma = pltpu.SemaphoreType.DMA
    rows = REQ_SECTION * QLEN
    part = rows // BLOCKS // 2
    width = ow.shape[1] // N_DEV
    return pl.pallas_call(
        back_kernel,
        out_shape=jax.ShapeDtypeStruct((rows, width), BF16),
        in_specs=[vmem, vmem, pl.BlockSpec(memory_space=pl.ANY)],
        out_specs=vmem,
        scratch_shapes=[
            pltpu.VMEM(ow.shape, BF16),
            pltpu.VMEM(o.shape[1:], BF16),
            pltpu.VMEM(lse.shape[1:], F32),
            pltpu.VMEM((rows, 2 * HD), BF16),
            pltpu.VMEM((BLOCKS, SIDE, SIDE, part, width), BF16),
            pltpu.VMEM((BLOCKS, SIDE, SIDE, part, width), BF16),
            pltpu.VMEM((BLOCKS, 2, 2, part, width), BF16),
            pltpu.VMEM((BLOCKS, 2, 2, part, width), BF16),
            pltpu.VMEM((BLOCKS, 2, SIDE, part, width), BF16),
            pltpu.VMEM((BLOCKS, 2, SIDE, part, width), BF16),
            pltpu.VMEM((BLOCKS, 2, SIDE, part, width), BF16),
            dma((1,)),
            dma((2,)),
            dma((2,)),
            dma((20 * BLOCKS,)),
            dma((20 * BLOCKS,)),
        ],
        compiler_params=pltpu.CompilerParams(
            collective_id=1, has_side_effects=True, vmem_limit_bytes=56 * 2**20
        ),
        name="back",
    )(o, lse, ow)


def body(
    activations, q_weight, out_weight, kv_weight, passage_store,
    passage_home, retrieved, slot_order, recomputed, passage_hidden,
):
    me = lax.axis_index("dev")
    per_device = passage_store.shape[1]
    home = passage_home[0][retrieved[0].reshape(SLOTS)]
    owners, store_slot = home // per_device, home % per_device
    offsets = slot_order[0].reshape(SLOTS) * PASS_LEN
    recomp = recomputed[0]
    earlier = jnp.arange(SLOTS)[None, :] < jnp.arange(SLOTS)[:, None]
    rank = jnp.sum(earlier & (owners[None, :] == owners[:, None]), axis=1)
    entry = (owners * CAP + rank).astype(jnp.int32)
    chosen = entry[None, :] == (me * CAP + jnp.arange(CAP))[:, None]

    def choose(values):
        shape = chosen.shape + (1,) * (values.ndim - 1)
        return jnp.sum(jnp.where(chosen.reshape(shape), values[None], 0), axis=1)

    rows = choose(store_slot).astype(jnp.int32)
    cos_s, sin_s = tables(choose(offsets))
    dropped = choose(recomp)
    index = jnp.arange(2 * HALF, dtype=jnp.int32)
    before = dropped - jnp.arange(RECOMP, dtype=jnp.int32)
    keep = index[None] + jnp.sum(before[:, :, None] <= index[None, None], axis=1)
    keep = keep.astype(jnp.int32)[:, :, None]
    sent = pack(rows, passage_store[0], keep, cos_s[:, None], sin_s[:, None])

    token_pos = TOPK * PASS_LEN + jnp.arange(QLEN, dtype=jnp.int32)
    cosq, sinq = tables(token_pos)
    q, kv, st = front(
        activations[0], passage_hidden[0], kv_weight[0], q_weight[0], sent, cosq, sinq
    )
    mine = lax.rem(me, 2).astype(jnp.int32)
    fresh_pos = jnp.pad(offsets[:, None] + recomp, ((0, 0), (0, PAD - RECOMP)))
    fresh_pos = jnp.where(mine == 0, fresh_pos[:TOPK], fresh_pos[TOPK:]).reshape(-1)
    cosk, sink = tables(jnp.concatenate([token_pos, fresh_pos]))
    valid = jnp.concatenate(
        [
            jnp.arange(HALF) < jnp.where(mine == 0, HALF, KEPT - HALF),
            jnp.arange(2 * PAD) % PAD < RECOMP,
        ]
    )
    bias = jnp.where(valid, 0.0, -jnp.inf).astype(F32)[:, None]
    o, lse = attend(
        entry, mine[None], q, kv, st.reshape(N_DEV * CAP, HALF, 2 * HD), cosk, sink, bias
    )
    return back(o, lse, out_weight[0])[None]


def solution(mesh):
    in_specs = (
        P("section", None, "dev"),
        P("section", None, "dev"),
        P("section", "dev", None),
        P("section", "dev", None),
        P("section", "dev", None, None, None),
        P("section", None),
        P("section", None, None),
        P("section", None, None),
        P("section", None, None),
        P("section", None, None, "dev"),
    )
    out_specs = P("section", None, "dev")
    return jax.shard_map(body, mesh=mesh, in_specs=in_specs, out_specs=out_specs, check_vma=False)
```

time: 586 us -> 253 us (0.43)
  waiting for transfers between devices: 437 us -> 0 us
  Pallas kernels: 0 us -> 230 us
  local copies, waits for them, and re-layouts: 58.1 us -> 12.4 us
  matrix products: 39.3 us -> 0 us
  other arithmetic: 24.1 us -> 5.95 us
  between operations: 13.4 us -> 0.23 us
  starting transfers between devices: 11.7 us -> 0 us
    unnamed x4 -> x0, waiting for transfers between devices: 286 us -> none
    pallas_call x0 -> x4, Pallas kernels: none -> 230 us  [the longest x1 139 us: front(): pl.pallas_call(front_kernel, out_shape=(jax.ShapeDtypeStruct((REQ_SECTION...]
    reduce_scatter x1 -> x0, waiting for transfers between devices: 84.4 us -> none  [body(): lax.psum_scatter(partial_out.astype(jnp.bfloat16), 'dev', scatter_dimensi...]
    all_gather x1 -> x0, waiting for transfers between devices: 50.9 us -> none  [body(): lax.all_gather(inputs, 'dev', axis=1, tiled=True)]
    dot_general x7 -> x0, matrix products: 39.3 us -> none  [the longest x1 8.75 us: body(): jnp.einsum('rqhd,rkd->rhqk', queries, context[..., :HD], preferred_elemen...]
    gather x3 -> x1, local copies, waits for them, and re-layouts: 19.9 us -> 0.66 us  [body(): home = passage_home[0][retrieved[0].reshape(SLOTS)]]
    unnamed x31 -> x20, local copies, waits for them, and re-layouts: 29.5 us -> 10.3 us
    ppermute x2 -> x0, waiting for transfers between devices: 15.7 us -> none  [the longest x1 9.24 us: partner_2(): return lax.ppermute(block, axis, route)]
  transfers between devices with their start and end apart: 6 -> 0, of which waited for: 5 -> 0; matrix products, arithmetic and copies ran while one was open for 7% -> 0% of each run, Pallas kernels for 0% -> 0%
where the time goes in v1:
time: 253 us; the launch traced here: 249 us
  Pallas kernels  230 us (91%)
  local copies, waits for them, and re-layouts  12.4 us (5%)
  other arithmetic  5.95 us (2%)
    pallas_call x1, Pallas kernels, front(): pl.pallas_call(front_kernel, out_shape=(jax.ShapeDtypeStruct((REQ_SECTION...  139 us
    pallas_call x1, Pallas kernels, back(): pl.pallas_call(back_kernel, out_shape=jax.ShapeDtypeStruct((rows, width),...  75.2 us
    pallas_call x1, Pallas kernels, attend(): pl.pallas_call(attend_kernel, out_shape=(jax.ShapeDtypeStruct((2, 2 * HD,...  12.3 us
    unnamed x20, local copies, waits for them, and re-layouts  10.3 us

profile of v1, /device:TPU:15, one launch (start us, length us, event | category | flops | bytes accessed | tf_op | source)
XLA Modules:
  0.0 248.7 jit_solution(10193509604762176758)
XLA Ops:
  0.0 0.8 reshape_squeeze.4
  0.8 0.7 gather_fusion
  1.5 0.2 convert_reduce_fusion
  1.7 0.7 broadcast_multiply_fusion
  2.4 0.1 mul.103
  2.5 0.2 select_reduce_fusion.1
  2.7 0.1 fusion.8
  2.8 0.1 pad_maximum_fusion.4
  2.8 0.8 select_reduce_fusion
  3.6 0.1 copy.23
  3.8 0.2 fusion
  4.0 0.2 copy.24
  4.3 0.0 copy-start.2
  4.3 3.4 %copy-done.2 = bf16[1,4,8,512,256]{4,3,2,1,0:T(8,128)(2,1)S(1)} copy-done((bf16[1,4,8,512,256]{4,3,2,1,0:T(8,128)(2,1)S(1)}, bf16[1,4,8,512,256]{4,3,2,1,0:T(8,128)(2,1)}, u32[]{:S(2)}) %copy-start.2) | copy-done | bytes 8388632
  7.7 3.9 %pack.1 = bf16[8,2,2,224,256]{4,3,2,1,0:T(8,128)(2,1)S(1)} custom-call(s32[2]{0:T(128)S(1)} %get-tuple-element.16.rows, bf16[4,8,512,256]{3,2,1,0:T(8,128)(2,1)S(1)} %bitcast.24, s32[2,448,1]{2,1,0:T(8,128)S(1)} %iota_add_fusion.keep, f32[2,1,128]{2,1,0:T(1,128)S(1)} %bitcast.25, f32[2,1,128]{2,1,0:T(1,128)S(1)} %bitcast.26), custom_call_target="tpu_custom_call" | custom-call | tf_op jit(solution)/shard_map/pack/pallas_call | solution.py:82
  11.5 1.8 copy-done.1
  13.3 0.5 fusion.2
  13.9 0.8 pad_maximum_fusion.2
  14.7 1.8 copy.28
  16.5 138.9 %front.1 = (bf16[2,4,256,128]{3,2,1,0:T(8,128)(2,1)}, bf16[896,256]{1,0:T(8,128)(2,1)}, bf16[16,2,224,256]{3,2,1,0:T(8,128)(2,1)}) custom-call(bf16[512,512]{1,0:T(8,128)(2,1)} %bitcast.33, bf16[16,77,512]{2,1,0:T(8,128)(2,1)} %bitcast.27, bf16[512,2048]{1,0:T(8,128)(2,1)} %bitcast.32, bf16[8192,256]{1,0:T(8,128)(2,1)} %bitcast.28, ...), custom_call_target="tpu_custom_call" | custom-call | tf_op jit(solution)/shard_map/front/pallas_call | solution.py:326
  155.4 0.1 broadcast_add_fusion
  155.5 0.1 concatenate.45
  155.6 1.7 fusion.1
  157.3 0.3 pad_maximum_fusion
  157.7 0.1 pad_add_fusion
  157.7 0.2 copy.26
  158.0 12.3 %attend.1 = (bf16[2,256,512]{2,1,0:T(8,128)(2,1)S(1)}, f32[2,8,512]{2,1,0:T(8,128)S(1)}) custom-call(s32[16]{0:T(128)S(1)} %multiply_add_fusion.entry, s32[1]{0:T(128)} %bitcast.2.mine, bf16[2,4,256,128]{3,2,1,0:T(8,128)(2,1)S(1)} %copy-done.3, bf16[896,256]{1,0:T(8,128)(2,1)S(1)} %copy-done.5, bf16[32,224,256]{2,1,0:T(8,128)(2,1)} %bitcast.30, ...), custom_call_target="tpu_custom_call" | custom-call | tf_op jit(solution)/shard_map/attend/pallas_call | solution.py:423
  170.3 0.0 copy-start.4
  170.3 0.8 copy-done.4
  171.1 0.6 copy-done.6
  171.7 75.2 %back.1 = bf16[512,512]{1,0:T(8,128)(2,1)} custom-call(bf16[2,256,512]{2,1,0:T(8,128)(2,1)} %copy-done.4, f32[2,8,512]{2,1,0:T(8,128)} %copy-done.6, bf16[256,8192]{1,0:T(8,128)(2,1)} %bitcast.29), custom_call_target="tpu_custom_call" | custom-call | tf_op jit(solution)/shard_map/back/pallas_call | solution.py:589
  246.9 1.9 copy.30
  (30 shorter events, 0.2 us)
Async XLA Ops:
  0.0 0.8 copy-start
  4.3 3.4 %copy-start.2 = (bf16[1,4,8,512,256]{4,3,2,1,0:T(8,128)(2,1)S(1)}, bf16[1,4,8,512,256]{4,3,2,1,0:T(8,128)(2,1)}, u32[]{:S(2)}) copy-start(bf16[1,4,8,512,256]{4,3,2,1,0:T(8,128)(2,1)} %param.14) | copy-start | bytes 25165828
  7.7 7.0 %copy-start.7 = (bf16[1,16,77,512]{3,1,2,0:T(8,128)(2,1)S(1)}, bf16[1,16,77,512]{3,1,2,0:T(8,128)(2,1)}, u32[]{:S(2)}) copy-start(bf16[1,16,77,512]{3,1,2,0:T(8,128)(2,1)} %param.19) | copy-start | bytes 3784708
  11.5 1.8 copy-start.1
  16.5 138.9 %copy-start.8 = (s32[1,16,77]{2,1,0:T(8,128)S(1)}, s32[1,16,77]{2,1,0:T(8,128)}, u32[]{:S(2)}) copy-start(s32[1,16,77]{2,1,0:T(8,128)} %param.18) | copy-start | bytes 14788
  155.4 2.6 %copy-start.3 = (bf16[2,4,256,128]{3,2,1,0:T(8,128)(2,1)S(1)}, bf16[2,4,256,128]{3,2,1,0:T(8,128)(2,1)}, u32[]{:S(2)}) copy-start(bf16[2,4,256,128]{3,2,1,0:T(8,128)(2,1)} %get-tuple-element.10.q) | copy-start | bytes 1572868
  155.4 2.6 %copy-start.5 = (bf16[896,256]{1,0:T(8,128)(2,1)S(1)}, bf16[896,256]{1,0:T(8,128)(2,1)}, u32[]{:S(2)}) copy-start(bf16[896,256]{1,0:T(8,128)(2,1)} %get-tuple-element.11.kv) | copy-start | bytes 1376260
  170.3 0.8 copy-start.4
  171.1 0.6 copy-start.6

commit v2 on v0

v2 whole, which is shorter than its diff:
```python
import functools

import jax
import jax.numpy as jnp
from jax import lax
from jax.experimental import pallas as pl
from jax.experimental.pallas import tpu as pltpu
from jax.sharding import PartitionSpec as P

QH = 32
KVH = 8
HD = 128
PASS_LEN = 512
TOPK = 8
RECOMP = 77
REQ_SECTION = 2
QLEN = 256
SLOTS = 16
CAP = 2
PASS_DEV = 4
SIDE = 4
N_DEV = 16
FRESH = 39
GROUP = QLEN + FRESH * SLOTS
FROWS = 320
KEPT = PASS_LEN - RECOMP
HALF = 224
PIECE = HALF // 2
BLOCKS = 4
ROPE_BASE = 500000.0
MESH = pl.DeviceIdType.MESH
F32 = jnp.float32
BF16 = jnp.bfloat16
SCALE = HD**-0.5 * 1.4426950408889634


def lane_tables(frequency, positions):
    angles = positions * frequency
    sign = jnp.where(lax.broadcasted_iota(jnp.int32, (1, HD), 1) < HD // 2, -1.0, 1.0)
    return jnp.cos(angles), jnp.sin(angles) * sign


def turned(v, cosine, sine):
    return v * cosine + pltpu.roll(v, HD // 2, axis=1) * sine


def place():
    d = lax.axis_index("dev")
    return lax.axis_index("section"), d // SIDE, lax.rem(d, SIDE)


def around(v, step):
    return lax.rem(v + step + SIDE, SIDE)


def remote(src, dst, send, recv, target):
    return pltpu.make_async_remote_copy(
        src_ref=src,
        dst_ref=dst,
        send_sem=send,
        recv_sem=recv,
        device_id=target,
        device_id_type=MESH,
    )


STEPS = (
    (0, 1), (0, 3), (1, 0), (3, 0), (1, 1), (3, 3), (1, 3), (3, 1),
    (0, 2), (2, 0), (2, 1), (2, 3), (1, 2), (3, 2), (2, 2),
)


def layer_kernel(
    home, retrieved, order, x, hid, kvw, qw, ow, store, rec, freq, pos, out,
    ent, xall, qv, kvv, rows, pa, pb, l1, r1, l2, r2, z2, qacc,
    storev, sent, st0, st1, q4, kf, vf, ko, vo, acc, m, l,
    oall, lall, oin, lin, wv, att, bl1, br1, bl2, br2, bz2, outv,
    loc, own_s, ag_s, ag_r, rs_s, rs_r, st_s, st_r, q_s, q_r, ex_s, ex_r, br_s, br_r,
):
    sec = lax.axis_index("section")
    me = lax.axis_index("dev")
    z, x_ = me // SIDE, lax.rem(me, SIDE)
    sections = lax.axis_size("section")
    after, before = lax.rem(sec + 1, sections), lax.rem(sec + sections - 1, sections)
    mine = lax.rem(me, 2)

    def at(zz, xx):
        return (sec, zz * SIDE + xx)

    right, left = at(z, around(x_, 1)), at(z, around(x_, -1))
    down, up = at(around(z, 1), x_), at(around(z, -1), x_)
    pair = (sec, me + 1 - 2 * mine)
    ahead = [(right, left), (down, up)]
    spot = [x_, z]

    greeted = [(sec, lax.rem(me + k, N_DEV)) for k in range(1, N_DEV)]
    for s in (after, before):
        greeted.append((s, me))
        for k in range(1, SIDE):
            greeted.append((s, z * SIDE + around(x_, k)))
            greeted.append((s, around(z, k) * SIDE + x_))
    barrier = pltpu.get_barrier_semaphore()
    for target in greeted:
        pl.semaphore_signal(barrier, inc=1, device_id=target, device_id_type=MESH)

    first_rows, last_rows = FRESH * SLOTS, (RECOMP - FRESH) * SLOTS
    loads = [
        pltpu.make_async_copy(kvw, kvv, loc.at[0]),
        pltpu.make_async_copy(x.at[pl.ds(0, QLEN)], rows.at[0, pl.ds(0, QLEN)], loc.at[1]),
        pltpu.make_async_copy(x.at[pl.ds(QLEN, QLEN)], rows.at[1, pl.ds(0, QLEN)], loc.at[2]),
        pltpu.make_async_copy(
            hid.at[pl.ds(0, first_rows)], rows.at[0, pl.ds(QLEN, first_rows)], loc.at[3]
        ),
        pltpu.make_async_copy(
            hid.at[pl.ds(first_rows, last_rows)], rows.at[1, pl.ds(QLEN, last_rows)], loc.at[4]
        ),
        pltpu.make_async_copy(store, storev, loc.at[5]),
        pltpu.make_async_copy(qw, qv, loc.at[6]),
        pltpu.make_async_copy(x.at[pl.ds(0, QLEN)], xall.at[0, me], loc.at[7]),
        pltpu.make_async_copy(x.at[pl.ds(QLEN, QLEN)], xall.at[1, me], loc.at[8]),
        pltpu.make_async_copy(ow, wv, loc.at[9]),
    ]
    for load in loads:
        load.start()
    rest = rows.at[1, pl.ds(QLEN + last_rows, GROUP - QLEN - last_rows)]
    rest[...] = jnp.zeros_like(rest)
    pl.semaphore_wait(barrier, len(greeted))

    def chunk(half, first, second):
        if half == 0:
            return around(z, second) * SIDE + around(x_, first)
        return around(z, first) * SIDE + around(x_, second)

    top, bottom = pl.ds(0, QLEN // 2), pl.ds(QLEN // 2, QLEN // 2)
    whole = pl.ds(0, QLEN)
    ag_sends, sends = [], []

    def ag(half, src, span, sem, target, own=False):
        to = xall.at[half, src, span]
        frm = x.at[pl.ds(half * QLEN, QLEN)] if own else to
        copy = remote(frm, to, ag_s.at[sem], ag_r.at[sem], target)
        copy.start()
        ag_sends.append(copy)

    def ag_wait(half, src, span, sem):
        to = xall.at[half, src, span]
        remote(to, to, ag_s.at[sem], ag_r.at[sem], right).wait_recv()

    for half in range(2):
        ag(half, me, whole, 20 * half, ahead[half][0], True)
        ag(half, me, whole, 20 * half + 1, ahead[half][1], True)
    for half in range(2):
        ag(half, me, whole, 20 * half + 4, ahead[1 - half][0], True)
        ag(half, me, whole, 20 * half + 5, ahead[1 - half][1], True)

    def push(group, src, dst, send, recv, target):
        copy = remote(src, dst, send, recv, target)
        copy.start()
        group.append(copy)

    def arrived(block, send, recv):
        remote(block, block, send, recv, right).wait_recv()

    def project(xx, zz):
        head = 2 * zz + xx // 2
        span = pl.ds(pl.multiple_of(head * 2 * HD, 2 * HD), 2 * HD)
        part = jnp.dot(rows[lax.rem(xx, 2)], kvv[:, span], preferred_element_type=F32)
        part = part.astype(BF16)
        pa[xx, zz] = part[:, :HD]
        pb[zz, xx] = part[:, HD:]

    def loop(count, step):
        def one(k, carry):
            step(k)
            return carry

        lax.fori_loop(0, count, one, 0)

    def skip_two(t):
        return t + t // 2

    parts = [pa, pb]
    lo, hi = pl.ds(0, 2), pl.ds(2, 2)

    def rs(half, src, dst, sem, target):
        push(sends, src, dst, rs_s.at[sem], rs_r.at[sem], target)

    def rs_first(half):
        p, c, b = parts[half], spot[half], 9 * half
        rs(half, p.at[around(c, 2), lo], l1.at[half], b, ahead[half][0])
        rs(half, p.at[around(c, 2), hi], r1.at[half], b + 1, ahead[half][1])

    for k in range(5):
        loads[k].wait()
    loop(SIDE, lambda k: project(around(x_, 2), around(z, k)))
    rs_first(0)
    loop(SIDE - 1, lambda k: project(around(x_, skip_two(k)), around(z, 2)))
    rs_first(1)
    loop(9, lambda k: project(around(x_, skip_two(k // 3)), around(z, skip_two(lax.rem(k, 3)))))
    for half in range(2):
        p, c, b = parts[half], spot[half], 9 * half
        rs(half, p.at[around(c, 1), hi], l2.at[half, hi], b + 2, ahead[half][0])
        rs(half, p.at[around(c, -1), lo], r2.at[half, lo], b + 3, ahead[half][1])

    for half in range(2):
        b = 20 * half
        src = chunk(half, -1, 0)
        ag_wait(half, src, whole, b)
        ag(half, src, top, b + 2, ahead[half][0])
        ag(half, src, whole, b + 8, ahead[1 - half][0])
        ag(half, src, whole, b + 9, ahead[1 - half][1])
        src = chunk(half, 1, 0)
        ag_wait(half, src, whole, b + 1)
        ag(half, src, bottom, b + 3, ahead[half][1])
        ag(half, src, whole, b + 12, ahead[1 - half][0])
        ag(half, src, whole, b + 13, ahead[1 - half][1])

    homes = [home[0, retrieved[0, j // TOPK, j % TOPK]] for j in range(SLOTS)]
    owners = [h // PASS_DEV for h in homes]
    entries = []
    for j in range(SLOTS):
        rank = jnp.int32(0)
        for i in range(j):
            rank = rank + jnp.where(owners[i] == owners[j], 1, 0)
        entries.append(owners[j] * CAP + rank)
        ent[j] = entries[j]
    frequency = freq[...]
    loads[5].wait()
    for c in range(CAP):
        row, slot, offset = jnp.int32(0), jnp.int32(0), jnp.int32(0)
        for j in range(SLOTS):
            hit = entries[j] == me * CAP + c
            row = jnp.where(hit, lax.rem(homes[j], PASS_DEV), row)
            slot = jnp.where(hit, j, slot)
            offset = jnp.where(hit, order[0, j // TOPK, j % TOPK] * PASS_LEN, offset)
        dropped = rec[0, pl.ds(slot, 1), :]
        ahead_of = (dropped - lax.broadcasted_iota(jnp.int32, (1, RECOMP), 1)).astype(F32)
        index = lax.broadcasted_iota(jnp.int32, (2 * HALF, RECOMP), 0).astype(F32)
        count = jnp.sum(jnp.where(ahead_of <= index, 1.0, 0.0), axis=1, keepdims=True)
        keep = index[:, :1] + count
        lanes = lax.broadcasted_iota(jnp.int32, (2 * HALF, PASS_LEN), 1).astype(F32)
        pick = jnp.where(lanes == keep, 1.0, 0.0).astype(BF16)
        cosine, sine = lane_tables(frequency, offset.astype(F32))

        def one_head(h):
            kept = jnp.dot(pick, storev[row, h], preferred_element_type=F32)
            keys = turned(kept[:, :HD], cosine, sine).astype(BF16)
            values = kept[:, HD:].astype(BF16)
            for half in range(2):
                for g in range(2):
                    start = half * HALF + g * PIECE
                    to = sent.at[g, 2 * h + half, c]
                    to[:, :HD] = keys[start : start + PIECE]
                    to[:, HD:] = values[start : start + PIECE]

        loop(KVH, one_head)

    st = [st0, st1]
    for g in range(2):
        copy = pltpu.make_async_copy(
            sent.at[g, me], st[g].at[pl.ds(2 * me, CAP)], own_s.at[g]
        )
        copy.start()

    def passages(g):
        for k, (dz, dx) in enumerate(STEPS):
            other = around(z, dz) * SIDE + around(x_, dx)
            sem = len(STEPS) * g + k
            push(sends, sent.at[g, other], st[g].at[pl.ds(2 * me, CAP)],
                 st_s.at[sem], st_r.at[sem], (sec, other))

    def passages_wait(g):
        pltpu.make_async_copy(
            sent.at[g, me], st[g].at[pl.ds(2 * me, CAP)], own_s.at[g]
        ).wait()
        for k, (dz, dx) in enumerate(STEPS):
            other = around(z, -dz) * SIDE + around(x_, -dx)
            sem = len(STEPS) * g + k
            arrived(st[g].at[pl.ds(2 * other, CAP)], st_s.at[sem], st_r.at[sem])

    for half in range(2):
        b = 20 * half
        src = chunk(half, 2, 0)
        ag_wait(half, src, top, b + 2)
        ag_wait(half, src, bottom, b + 3)
        ag(half, src, whole, b + 16, ahead[1 - half][0])
        ag(half, src, whole, b + 17, ahead[1 - half][1])

    def second_axis(k, first):
        for half in range(2):
            b = 20 * half + 4 + 4 * k
            src = chunk(half, first, -1)
            ag_wait(half, src, whole, b)
            ag(half, src, top, b + 2, ahead[1 - half][0])
            src = chunk(half, first, 1)
            ag_wait(half, src, whole, b + 1)
            ag(half, src, bottom, b + 3, ahead[1 - half][1])

    second_axis(0, 0)

    for half in range(2):
        p, c, b = parts[half], spot[half], 9 * half
        arrived(l1.at[half], rs_s.at[b], rs_r.at[b])
        for u in range(2):
            block = p.at[around(c, 1), u]
            block[...] = (block[...].astype(F32) + l1[half, u].astype(F32)).astype(BF16)
        rs(half, p.at[around(c, 1), lo], l2.at[half, lo], b + 4, ahead[half][0])
        arrived(r1.at[half], rs_s.at[b + 1], rs_r.at[b + 1])
        for u in range(2):
            block = p.at[around(c, -1), 2 + u]
            block[...] = (block[...].astype(F32) + r1[half, u].astype(F32)).astype(BF16)
        rs(half, p.at[around(c, -1), hi], r2.at[half, hi], b + 5, ahead[half][1])

    second_axis(1, -1)
    second_axis(2, 1)
    passages(0)
    second_axis(3, 2)

    for half in range(2):
        p, c, b = parts[half], spot[half], 9 * half
        arrived(l2.at[half, hi], rs_s.at[b + 2], rs_r.at[b + 2])
        arrived(r2.at[half, lo], rs_s.at[b + 3], rs_r.at[b + 3])
        arrived(l2.at[half, lo], rs_s.at[b + 4], rs_r.at[b + 4])
        arrived(r2.at[half, hi], rs_s.at[b + 5], rs_r.at[b + 5])
        for u in range(SIDE):
            block = p.at[c, u]
            total = block[...].astype(F32) + l2[half, u].astype(F32) + r2[half, u].astype(F32)
            block[...] = total.astype(BF16)
        for k in (1, 3, 2):
            other = around(spot[1 - half], k)
            target = at(other, x_) if half == 0 else at(z, other)
            rs(half, p.at[c, other], z2.at[half, k - 1], b + 5 + k, target)
    passages(1)

    for k in (6, 7, 8):
        loads[k].wait()
    for half in range(2):
        for k in range(SIDE):
            b = 20 * half + 4 + 4 * k
            src = chunk(half, (0, -1, 1, 2)[k], 2)
            ag_wait(half, src, top, b + 2)
            ag_wait(half, src, bottom, b + 3)

    def project_queries(k):
        span = pl.ds(pl.multiple_of(k * 2 * QLEN, 2 * QLEN), 2 * QLEN)
        weight = qv[span, :]
        for half in range(2):
            qacc[half] += jnp.dot(xall[half, k], weight, preferred_element_type=F32)

    qacc[...] = jnp.zeros_like(qacc)
    loop(N_DEV, project_queries)
    token_at = lax.broadcasted_iota(jnp.int32, (QLEN, 1), 0) + TOPK * PASS_LEN
    cosine, sine = lane_tables(frequency, token_at.astype(F32))
    base = 2 * mine
    for half in range(2):
        for j in range(2):
            head = turned(qacc[half, :, j * HD : (j + 1) * HD], cosine, sine)
            q4[half, base + j] = head.astype(BF16)
        block = q4.at[half, pl.ds(base, 2)]
        push(sends, block, block, q_s.at[half], q_r.at[half], pair)

    cosine, sine = lane_tables(frequency, pos[...])
    for half in range(2):
        p, c, b = parts[half], spot[half], 9 * half
        total = p[c, spot[1 - half]].astype(F32)
        for k in range(1, SIDE):
            block = z2.at[half, k - 1]
            arrived(block, rs_s.at[b + 5 + k], rs_r.at[b + 5 + k])
            total += block[...].astype(F32)
        total = total.astype(BF16).astype(F32)
        if half == 0:
            total = turned(total, cosine, sine)
        own_to, fresh_to = (ko, kf) if half == 0 else (vo, vf)
        own_to[...] = total[:QLEN].astype(BF16)
        fresh = total[QLEN:].reshape(FRESH, SLOTS, HD)
        for r in range(REQ_SECTION):
            rows_of = fresh[:, r * TOPK : (r + 1) * TOPK].reshape(FRESH * TOPK, HD)
            filler = jnp.zeros((FROWS - FRESH * TOPK, HD), F32)
            fresh_to[r] = jnp.concatenate([rows_of, filler], axis=0).astype(BF16)

    cols = 4 * QLEN

    def score(keys, queries):
        s = lax.dot_general(
            keys, queries, (((1,), (1,)), ((), ())), preferred_element_type=F32
        )
        return s * SCALE

    def update(r, scores, values):
        old = m[r]
        new = old
        for s in scores:
            new = jnp.maximum(new, jnp.max(s, axis=0, keepdims=True))
        scale = jnp.exp2(old - new)
        total, mixed = l[r] * scale, acc[r] * scale
        for s, v in zip(scores, values):
            weights = jnp.exp2(s - new)
            total = total + jnp.sum(weights, axis=0, keepdims=True)
            mixed = mixed + lax.dot_general(
                v, weights.astype(BF16), (((0,), (0,)), ((), ())), preferred_element_type=F32
            )
        m[r], l[r], acc[r] = new, total, mixed

    def bias(count, valid):
        index = lax.broadcasted_iota(jnp.int32, (count, 1), 0)
        return jnp.where(index < valid, 0.0, -jnp.inf)

    def queries_of(r):
        return q4[r].reshape(cols, HD)

    def stored(r, g):
        def two(k):
            scores, values = [], []
            for i in range(2):
                e = ent[r * TOPK + 2 * k + i]
                block = st[g].at[e]
                s = score(block[:, :HD], queries_of(r))
                if g == 1:
                    s = s + bias(PIECE, KEPT - HALF - PIECE + (2 * HALF - KEPT) * (1 - mine))
                scores.append(s)
                values.append(block[:, HD:])
            update(r, scores, values)

        loop(TOPK // 2, two)

    for half in range(2):
        block = q4.at[half, pl.ds(2 - base, 2)]
        arrived(block, q_s.at[half], q_r.at[half])
    m[...] = jnp.full_like(m, -1e30)
    l[...] = jnp.zeros_like(l)
    acc[...] = jnp.zeros_like(acc)
    for r in range(REQ_SECTION):
        s = score(kf[r], queries_of(r)) + bias(FROWS, FRESH * TOPK - TOPK * mine)
        update(r, [s], [vf[r]])
    s = score(ko[...], queries_of(mine))
    keys_at = lax.broadcasted_iota(jnp.int32, (QLEN, cols), 0)
    query_at = lax.rem(lax.broadcasted_iota(jnp.int32, (QLEN, cols), 1), QLEN)
    s = jnp.where(keys_at <= query_at, s, -jnp.inf)
    update(mine, [s], [vo[...]])

    def finish(r):
        done = (acc[r] / l[r]).astype(BF16)
        level = m[r] + jnp.log2(l[r])
        for j in range(4):
            span = slice(j * QLEN, (j + 1) * QLEN)
            oall[r, j // 2, pl.ds((j % 2) * HD, HD), :] = done[:, span]
            lall[r, j // 2, pl.ds(j % 2, 1), :] = level[:, span]
        push(sends, oall.at[r, 1 - mine], oin.at[r], ex_s.at[2 * r], ex_r.at[2 * r], pair)
        push(sends, lall.at[r, 1 - mine], lin.at[r], ex_s.at[2 * r + 1], ex_r.at[2 * r + 1], pair)

    def join(r):
        arrived(oin.at[r], ex_s.at[2 * r], ex_r.at[2 * r])
        arrived(lin.at[r], ex_s.at[2 * r + 1], ex_r.at[2 * r + 1])
        for j in range(2):
            a, b = lall[r, mine, pl.ds(j, 1), :], lin[r, pl.ds(j, 1), :]
            most = jnp.maximum(a, b)
            a, b = jnp.exp2(a - most), jnp.exp2(b - most)
            span = pl.ds(j * HD, HD)
            joined = oall[r, mine, span, :].astype(F32) * a + oin[r, span, :].astype(F32) * b
            joined = joined / (a + b)
            att[r * QLEN : (r + 1) * QLEN, j * HD : (j + 1) * HD] = joined.T.astype(BF16)

    size = REQ_SECTION * QLEN // BLOCKS
    part = size // 2
    width = xall.shape[3]

    def units(b, half, first, second, count):
        return xall.at[half, pl.ds(first * SIDE + second, count), pl.ds(b * part, part)]

    def compute(b):
        def one(k):
            xx = around(x_, 2 + k // SIDE)
            zz = around(z, 2 + lax.rem(k, SIDE))
            span = pl.ds(pl.multiple_of((zz * SIDE + xx) * width, width), width)
            got = jnp.dot(
                att[b * size : (b + 1) * size, :], wv[:, span], preferred_element_type=F32
            ).astype(BF16)
            xall[0, xx * SIDE + zz, pl.ds(b * part, part)] = got[:part]
            xall[1, zz * SIDE + xx, pl.ds(b * part, part)] = got[part:]

        loop(N_DEV, one)

    def out_push(s, src, dst, target):
        push(sends, src, dst, br_s.at[s], br_r.at[s], target)

    def first(b):
        for half in range(2):
            c, s = spot[half], 20 * b + 10 * half
            out_push(s, units(b, half, around(c, 2), 0, 2), bl1.at[b, half], ahead[half][0])
            out_push(s + 1, units(b, half, around(c, 2), 2, 2), br1.at[b, half], ahead[half][1])
            out_push(s + 2, units(b, half, around(c, 1), 2, 2), bl2.at[b, half, hi], ahead[half][0])
            out_push(s + 3, units(b, half, around(c, -1), 0, 2), br2.at[b, half, lo], ahead[half][1])

    def out_arrived(block, s):
        arrived(block, br_s.at[s], br_r.at[s])

    def second(b):
        for half in range(2):
            c, s = spot[half], 20 * b + 10 * half
            out_arrived(bl1.at[b, half], s)
            block = units(b, half, around(c, 1), 0, 2)
            block[...] = (block[...].astype(F32) + bl1[b, half].astype(F32)).astype(BF16)
            out_push(s + 4, block, bl2.at[b, half, lo], ahead[half][0])
            out_arrived(br1.at[b, half], s + 1)
            block = units(b, half, around(c, -1), 2, 2)
            block[...] = (block[...].astype(F32) + br1[b, half].astype(F32)).astype(BF16)
            out_push(s + 5, block, br2.at[b, half, hi], ahead[half][1])

    def third(b):
        for half in range(2):
            c, s = spot[half], 20 * b + 10 * half
            out_arrived(bl2.at[b, half, hi], s + 2)
            out_arrived(br2.at[b, half, lo], s + 3)
            out_arrived(bl2.at[b, half, lo], s + 4)
            out_arrived(br2.at[b, half, hi], s + 5)
            block = units(b, half, c, 0, SIDE)
            total = block[...].astype(F32) + bl2[b, half].astype(F32) + br2[b, half].astype(F32)
            block[...] = total.astype(BF16)
            for k in (1, 3, 2, 0):
                other = around(spot[1 - half], k)
                target = (after, other * SIDE + x_) if half == 0 else (after, z * SIDE + other)
                out_push(s + 6 + k, xall.at[half, c * SIDE + other, pl.ds(b * part, part)],
                         bz2.at[b, half, k], target)

    def fourth(b):
        for half in range(2):
            s = 20 * b + 10 * half
            total = None
            for k in range(SIDE):
                out_arrived(bz2.at[b, half, k], s + 6 + k)
                block = bz2[b, half, k].astype(F32)
                total = block if total is None else total + block
            outv[pl.ds(b * size + half * part, part), :] = total.astype(BF16)

    passages_wait(0)
    stored(0, 0)
    stored(1, 0)
    for copy in ag_sends:
        copy.wait_send()
    loads[9].wait()
    passages_wait(1)
    stored(0, 1)
    finish(0)
    stored(1, 1)
    finish(1)
    join(0)
    per = BLOCKS // REQ_SECTION
    for b in range(per):
        compute(b)
        first(b)
    join(1)
    for b in range(BLOCKS):
        if per + b < BLOCKS:
            compute(per + b)
            first(per + b)
        second(b)
        if b > 0:
            third(b - 1)
    third(BLOCKS - 1)
    for b in range(BLOCKS):
        fourth(b)
    done = pltpu.make_async_copy(outv, out, loc.at[10])
    done.start()
    for copy in sends:
        copy.wait_send()
    done.wait()


def layer(home, retrieved, order, x, hid, kvw, qw, ow, store, rec, freq, pos):
    anywhere = pl.BlockSpec(memory_space=pl.ANY)
    vmem = pl.BlockSpec(memory_space=pltpu.VMEM)
    smem = pl.BlockSpec(memory_space=pltpu.SMEM)
    dma = pltpu.SemaphoreType.DMA
    d_here = x.shape[1]
    cols = 4 * QLEN
    part = REQ_SECTION * QLEN // BLOCKS // 2
    width = ow.shape[1] // N_DEV
    assert width == d_here

    def bf16(*shape):
        return pltpu.VMEM(shape, BF16)

    def f32(*shape):
        return pltpu.VMEM(shape, F32)

    return pl.pallas_call(
        layer_kernel,
        out_shape=jax.ShapeDtypeStruct((REQ_SECTION * QLEN, width), BF16),
        in_specs=[smem] * 3 + [anywhere] * 6 + [vmem] * 3,
        out_specs=anywhere,
        scratch_shapes=[
            pltpu.SMEM((SLOTS,), jnp.int32),
            bf16(2, N_DEV, QLEN, d_here),
            bf16(*qw.shape),
            bf16(*kvw.shape),
            bf16(REQ_SECTION, GROUP, d_here),
            bf16(SIDE, SIDE, GROUP, HD),
            bf16(SIDE, SIDE, GROUP, HD),
            bf16(2, 2, GROUP, HD),
            bf16(2, 2, GROUP, HD),
            bf16(2, SIDE, GROUP, HD),
            bf16(2, SIDE, GROUP, HD),
            bf16(2, SIDE - 1, GROUP, HD),
            f32(2, QLEN, 2 * HD),
            bf16(*store.shape),
            bf16(2, N_DEV, CAP, PIECE, 2 * HD),
            bf16(N_DEV * CAP, PIECE, 2 * HD),
            bf16(N_DEV * CAP, PIECE, 2 * HD),
            bf16(REQ_SECTION, 4, QLEN, HD),
            bf16(REQ_SECTION, FROWS, HD),
            bf16(REQ_SECTION, FROWS, HD),
            bf16(QLEN, HD),
            bf16(QLEN, HD),
            f32(REQ_SECTION, HD, cols),
            f32(REQ_SECTION, 1, cols),
            f32(REQ_SECTION, 1, cols),
            bf16(REQ_SECTION, 2, 2 * HD, QLEN),
            f32(REQ_SECTION, 2, 8, QLEN),
            bf16(REQ_SECTION, 2 * HD, QLEN),
            f32(REQ_SECTION, 8, QLEN),
            bf16(*ow.shape),
            bf16(REQ_SECTION * QLEN, 2 * HD),
            bf16(BLOCKS, 2, 2, part, width),
            bf16(BLOCKS, 2, 2, part, width),
            bf16(BLOCKS, 2, SIDE, part, width),
            bf16(BLOCKS, 2, SIDE, part, width),
            bf16(BLOCKS, 2, SIDE, part, width),
            bf16(REQ_SECTION * QLEN, width),
            dma((11,)),
            dma((2,)),
            dma((40,)),
            dma((40,)),
            dma((18,)),
            dma((18,)),
            dma((2 * len(STEPS),)),
            dma((2 * len(STEPS),)),
            dma((2,)),
            dma((2,)),
            dma((4,)),
            dma((4,)),
            dma((20 * BLOCKS,)),
            dma((20 * BLOCKS,)),
        ],
        compiler_params=pltpu.CompilerParams(
            collective_id=0, has_side_effects=True, vmem_limit_bytes=63 * 2**20
        ),
        name="layer",
    )(home, retrieved, order, x, hid, kvw, qw, ow, store, rec, freq, pos)


def body(
    activations, q_weight, out_weight, kv_weight, passage_store,
    passage_home, retrieved, slot_order, recomputed, passage_hidden,
):
    mine = lax.rem(lax.axis_index("dev"), 2)
    half_dim = HD // 2
    frequency = ROPE_BASE ** (-(jnp.arange(half_dim, dtype=F32) * (2.0 / HD)))
    frequency = jnp.concatenate([frequency, frequency])[None]
    offsets = slot_order[0].reshape(SLOTS) * PASS_LEN
    fresh_pos = jnp.pad(recomputed[0].T + offsets, ((0, 2 * FRESH - RECOMP), (0, 0)))
    fresh_pos = jnp.where(mine == 0, fresh_pos[:FRESH], fresh_pos[FRESH:]).reshape(-1)
    token_pos = TOPK * PASS_LEN + jnp.arange(QLEN, dtype=jnp.int32)
    pos = jnp.concatenate([token_pos, fresh_pos]).astype(F32)[:, None]
    hidden = passage_hidden[0].transpose(1, 0, 2).reshape(RECOMP * SLOTS, -1)
    out = layer(
        passage_home, retrieved, slot_order, activations[0], hidden, kv_weight[0], q_weight[0],
        out_weight[0], passage_store[0], recomputed, frequency, pos,
    )
    return out[None]


def solution(mesh):
    in_specs = (
        P("section", None, "dev"),
        P("section", None, "dev"),
        P("section", "dev", None),
        P("section", "dev", None),
        P("section", "dev", None, None, None),
        P("section", None),
        P("section", None, None),
        P("section", None, None),
        P("section", None, None),
        P("section", None, None, "dev"),
    )
    out_specs = P("section", None, "dev")
    return jax.shard_map(body, mesh=mesh, in_specs=in_specs, out_specs=out_specs, check_vma=False)
```

time: 586 us -> 221 us (0.38)
  waiting for transfers between devices: 437 us -> 0 us
  Pallas kernels: 0 us -> 215 us
  local copies, waits for them, and re-layouts: 58.1 us -> 3.12 us
  matrix products: 39.3 us -> 0 us
  other arithmetic: 24.1 us -> 2.22 us
  between operations: 13.4 us -> 0.02 us
  starting transfers between devices: 11.7 us -> 0 us
    unnamed x4 -> x0, waiting for transfers between devices: 286 us -> none
    pallas_call x0 -> x1, Pallas kernels: none -> 215 us  [layer(): pl.pallas_call(layer_kernel, out_shape=jax.ShapeDtypeStruct((REQ_SECTION...]
    reduce_scatter x1 -> x0, waiting for transfers between devices: 84.4 us -> none  [body(): lax.psum_scatter(partial_out.astype(jnp.bfloat16), 'dev', scatter_dimensi...]
    all_gather x1 -> x0, waiting for transfers between devices: 50.9 us -> none  [body(): lax.all_gather(inputs, 'dev', axis=1, tiled=True)]
    dot_general x7 -> x0, matrix products: 39.3 us -> none  [the longest x1 8.75 us: body(): jnp.einsum('rqhd,rkd->rhqk', queries, context[..., :HD], preferred_elemen...]
    unnamed x31 -> x1, local copies, waits for them, and re-layouts: 29.5 us -> 1.87 us
    gather x3 -> x0, local copies, waits for them, and re-layouts: 19.9 us -> none  [the longest x1 10.7 us: body(): outgoing = store_here[:, dest_heads]]
    ppermute x2 -> x0, waiting for transfers between devices: 15.7 us -> none  [the longest x1 9.24 us: partner_2(): return lax.ppermute(block, axis, route)]
  transfers between devices with their start and end apart: 6 -> 0, of which waited for: 5 -> 0; matrix products, arithmetic and copies ran while one was open for 7% -> 0% of each run, Pallas kernels for 0% -> 0%
where the time goes in v2:
time: 221 us
  Pallas kernels  215 us (97%)
  local copies, waits for them, and re-layouts  3.12 us (1%)
  other arithmetic  2.22 us (1%)
    pallas_call x1, Pallas kernels, layer(): pl.pallas_call(layer_kernel, out_shape=jax.ShapeDtypeStruct((REQ_SECTION...  215 us

profile of v2, /device:TPU:15, one launch (start us, length us, event | category | flops | bytes accessed | tf_op | source)
XLA Modules:
  0.0 220.6 jit_solution(10651275217688917287)
XLA Ops:
  0.0 0.7 maximum_bitcast_fusion.freq
  0.7 0.7 broadcast_multiply_fusion
  1.4 0.1 mul.21
  1.5 0.8 fusion
  2.2 0.1 slice_select_fusion
  2.3 0.1 copy.17
  2.4 0.1 concatenate.19
  2.5 1.0 copy.18.pos
  3.5 215.3 %layer.1 = bf16[512,512]{1,0:T(8,128)(2,1)} custom-call(s32[1,64]{1,0:T(1,128)} %home.1, s32[1,2,8]{2,1,0:T(2,128)} %retrieved.1, s32[1,2,8]{2,1,0:T(2,128)} %order.1, bf16[512,512]{1,0:T(8,128)(2,1)} %bitcast.26, bf16[1232,512]{1,0:T(8,128)(2,1)} %bitcast.25, bf16[512,2048]{1,0:T(8,128)(2,1)} %bitcast.23, bf16[8192,256]{1,0:T(8,128)(2,1)} %bitcast.21, ...), custom_call_target="tpu_custom_call" | custom-call | tf_op jit(solution)/shard_map/layer/pallas_call | solution.py:586
  218.8 1.9 copy.20
  (3 shorter events, 0.0 us)

commit v3 on v2

v3 whole, which is shorter than its diff:
```python
import functools

import jax
import jax.numpy as jnp
import numpy as np
from jax import lax
from jax.experimental import pallas as pl
from jax.experimental.pallas import tpu as pltpu
from jax.sharding import PartitionSpec as P

QH = 32
KVH = 8
HD = 128
PASS_LEN = 512
TOPK = 8
RECOMP = 77
REQ_SECTION = 2
QLEN = 256
SLOTS = 16
CAP = 2
PASS_DEV = 4
SIDE = 4
N_DEV = 16
FRESH = 39
GROUP = QLEN + FRESH * SLOTS
FROWS = 320
KEPT = PASS_LEN - RECOMP
HALF = 224
PIECES = (112, 64, 48)
STARTS = (0, 112, 176)
GROUPS = len(PIECES)
BLOCKS = 4
ROPE_BASE = 500000.0
MESH = pl.DeviceIdType.MESH
F32 = jnp.float32
BF16 = jnp.bfloat16
SCALE = HD**-0.5 * 1.4426950408889634


def lane_tables(angles):
    sign = jnp.where(lax.broadcasted_iota(jnp.int32, (1, HD), 1) < HD // 2, -1.0, 1.0)
    return jnp.cos(angles), jnp.sin(angles) * sign


def turned(v, cosine, sine):
    return v * cosine + pltpu.roll(v, HD // 2, axis=1) * sine


def place():
    d = lax.axis_index("dev")
    return lax.axis_index("section"), d // SIDE, lax.rem(d, SIDE)


def around(v, step):
    return lax.rem(v + step + SIDE, SIDE)


def remote(src, dst, send, recv, target):
    return pltpu.make_async_remote_copy(
        src_ref=src,
        dst_ref=dst,
        send_sem=send,
        recv_sem=recv,
        device_id=target,
        device_id_type=MESH,
    )


STEPS = (
    (0, 1), (0, 3), (1, 0), (3, 0), (1, 1), (3, 3), (1, 3), (3, 1),
    (0, 2), (2, 0), (2, 1), (2, 3), (1, 2), (3, 2), (2, 2),
)


def layer_kernel(
    home, retrieved, order, x, hid, kvw, qw, ow, store, rec, freq, out,
    ent, xall, qv, kvv, rows, pa, pb, l1, r1, l2, r2, z2, qacc,
    storev, out0, out1, out2, st0, st1, st2, q4, kf, vf, ko, vo, acc, m, l,
    angle, oall, lall, oin, lin, wv, att, bl1, br1, bl2, br2, bz2, outv,
    loc, own_s, ag_s, ag_r, rs_s, rs_r, st_s, st_r, q_s, q_r, ex_s, ex_r, br_s, br_r,
):
    sec = lax.axis_index("section")
    me = lax.axis_index("dev")
    z, x_ = me // SIDE, lax.rem(me, SIDE)
    sections = lax.axis_size("section")
    after, before = lax.rem(sec + 1, sections), lax.rem(sec + sections - 1, sections)
    mine = lax.rem(me, 2)

    def at(zz, xx):
        return (sec, zz * SIDE + xx)

    right, left = at(z, around(x_, 1)), at(z, around(x_, -1))
    down, up = at(around(z, 1), x_), at(around(z, -1), x_)
    pair = (sec, me + 1 - 2 * mine)
    ahead = [(right, left), (down, up)]
    spot = [x_, z]

    greeted = [(sec, lax.rem(me + k, N_DEV)) for k in range(1, N_DEV)]
    for s in (after, before):
        greeted.append((s, me))
        for k in range(1, SIDE):
            greeted.append((s, z * SIDE + around(x_, k)))
            greeted.append((s, around(z, k) * SIDE + x_))
    barrier = pltpu.get_barrier_semaphore()
    for target in greeted:
        pl.semaphore_signal(barrier, inc=1, device_id=target, device_id_type=MESH)

    first_rows, last_rows = FRESH * SLOTS, (RECOMP - FRESH) * SLOTS
    loads = [
        pltpu.make_async_copy(kvw, kvv, loc.at[0]),
        pltpu.make_async_copy(x.at[pl.ds(0, QLEN)], rows.at[0, pl.ds(0, QLEN)], loc.at[1]),
        pltpu.make_async_copy(x.at[pl.ds(QLEN, QLEN)], rows.at[1, pl.ds(0, QLEN)], loc.at[2]),
        pltpu.make_async_copy(
            hid.at[pl.ds(0, first_rows)], rows.at[0, pl.ds(QLEN, first_rows)], loc.at[3]
        ),
        pltpu.make_async_copy(
            hid.at[pl.ds(first_rows, last_rows)], rows.at[1, pl.ds(QLEN, last_rows)], loc.at[4]
        ),
        pltpu.make_async_copy(store, storev, loc.at[5]),
        pltpu.make_async_copy(qw, qv, loc.at[6]),
        pltpu.make_async_copy(x.at[pl.ds(0, QLEN)], xall.at[0, me], loc.at[7]),
        pltpu.make_async_copy(x.at[pl.ds(QLEN, QLEN)], xall.at[1, me], loc.at[8]),
        pltpu.make_async_copy(ow, wv, loc.at[9]),
    ]
    for load in loads:
        load.start()
    rest = rows.at[1, pl.ds(QLEN + last_rows, GROUP - QLEN - last_rows)]
    rest[...] = jnp.zeros_like(rest)
    pl.semaphore_wait(barrier, len(greeted))

    def chunk(half, first, second):
        if half == 0:
            return around(z, second) * SIDE + around(x_, first)
        return around(z, first) * SIDE + around(x_, second)

    top, bottom = pl.ds(0, QLEN // 2), pl.ds(QLEN // 2, QLEN // 2)
    whole = pl.ds(0, QLEN)
    sends = []

    def ag(half, src, span, sem, target, own=False):
        to = xall.at[half, src, span]
        frm = x.at[pl.ds(half * QLEN, QLEN)] if own else to
        remote(frm, to, ag_s.at[half], ag_r.at[15 * half + sem], target).start()

    def ag_wait(half, src, sem):
        to = xall.at[half, src, whole]
        remote(to, to, ag_s.at[half], ag_r.at[15 * half + sem], right).wait_recv()

    for half in range(2):
        ag(half, me, whole, 0, ahead[half][0], True)
        ag(half, me, whole, 1, ahead[half][1], True)
    for half in range(2):
        ag(half, me, whole, 3, ahead[1 - half][0], True)
        ag(half, me, whole, 4, ahead[1 - half][1], True)

    def push(group, src, dst, send, recv, target):
        copy = remote(src, dst, send, recv, target)
        copy.start()
        group.append(copy)

    def arrived(block, send, recv):
        remote(block, block, send, recv, right).wait_recv()

    def project(xx, zz):
        head = 2 * zz + xx // 2
        span = pl.ds(pl.multiple_of(head * 2 * HD, 2 * HD), 2 * HD)
        part = jnp.dot(rows[lax.rem(xx, 2)], kvv[:, span], preferred_element_type=F32)
        part = part.astype(BF16)
        pa[xx, zz] = part[:, :HD]
        pb[zz, xx] = part[:, HD:]

    def loop(count, step):
        def one(k, carry):
            step(k)
            return carry

        lax.fori_loop(0, count, one, 0)

    def skip_two(t):
        return t + t // 2

    parts = [pa, pb]
    lo, hi = pl.ds(0, 2), pl.ds(2, 2)

    def rs(half, src, dst, sem, target):
        remote(src, dst, rs_s.at[2 * half + sem // 4], rs_r.at[5 * half + sem], target).start()

    def rs_arrived(half, block, sem):
        arrived(block, rs_s.at[2 * half + sem // 4], rs_r.at[5 * half + sem])

    def rs_first(half):
        p, c = parts[half], spot[half]
        rs(half, p.at[around(c, 2), lo], l1.at[half], 0, ahead[half][0])
        rs(half, p.at[around(c, 2), hi], r1.at[half], 1, ahead[half][1])

    for k in range(5):
        loads[k].wait()
    loop(SIDE, lambda k: project(around(x_, 2), around(z, k)))
    rs_first(0)
    loop(SIDE - 1, lambda k: project(around(x_, skip_two(k)), around(z, 2)))
    rs_first(1)
    loop(9, lambda k: project(around(x_, skip_two(k // 3)), around(z, skip_two(lax.rem(k, 3)))))

    for half in range(2):
        src = chunk(half, -1, 0)
        ag_wait(half, src, 0)
        ag(half, src, top, 2, ahead[half][0])
        ag(half, src, whole, 6, ahead[1 - half][0])
        ag(half, src, whole, 7, ahead[1 - half][1])
        src = chunk(half, 1, 0)
        ag_wait(half, src, 1)
        ag(half, src, bottom, 2, ahead[half][1])
        ag(half, src, whole, 9, ahead[1 - half][0])
        ag(half, src, whole, 10, ahead[1 - half][1])
    for half in range(2):
        p, c = parts[half], spot[half]
        rs(half, p.at[around(c, 1), hi], l2.at[half, hi], 2, ahead[half][0])
        rs(half, p.at[around(c, -1), lo], r2.at[half, lo], 3, ahead[half][1])

    homes = [home[0, retrieved[0, j // TOPK, j % TOPK]] for j in range(SLOTS)]
    owners = [h // PASS_DEV for h in homes]
    entries = []
    for j in range(SLOTS):
        rank = jnp.int32(0)
        for i in range(j):
            rank = rank + jnp.where(owners[i] == owners[j], 1, 0)
        entries.append(owners[j] * CAP + rank)
        ent[j] = entries[j]
    frequency = freq[...]
    sent, st = [out0, out1, out2], [st0, st1, st2]
    loads[5].wait()
    for c in range(CAP):
        row, slot, offset = jnp.int32(0), jnp.int32(0), jnp.int32(0)
        for j in range(SLOTS):
            hit = entries[j] == me * CAP + c
            row = jnp.where(hit, lax.rem(homes[j], PASS_DEV), row)
            slot = jnp.where(hit, j, slot)
            offset = jnp.where(hit, order[0, j // TOPK, j % TOPK] * PASS_LEN, offset)
        dropped = rec[0, pl.ds(slot, 1), :]
        ahead_of = (dropped - lax.broadcasted_iota(jnp.int32, (1, RECOMP), 1)).astype(F32)
        index = lax.broadcasted_iota(jnp.int32, (2 * HALF, RECOMP), 0).astype(F32)
        count = jnp.sum(jnp.where(ahead_of <= index, 1.0, 0.0), axis=1, keepdims=True)
        keep = index[:, :1] + count
        lanes = lax.broadcasted_iota(jnp.int32, (2 * HALF, PASS_LEN), 1).astype(F32)
        pick = jnp.where(lanes == keep, 1.0, 0.0).astype(BF16)
        cosine, sine = lane_tables(frequency * offset.astype(F32))

        def one_head(h):
            kept = jnp.dot(pick, storev[row, h], preferred_element_type=F32)
            keys = turned(kept[:, :HD], cosine, sine).astype(BF16)
            values = kept[:, HD:].astype(BF16)
            for half in range(2):
                for g in range(GROUPS):
                    start = half * HALF + STARTS[g]
                    to = sent[g].at[2 * h + half, c]
                    to[:, :HD] = keys[start : start + PIECES[g]]
                    to[:, HD:] = values[start : start + PIECES[g]]

        loop(KVH, one_head)

    for g in range(GROUPS):
        copy = pltpu.make_async_copy(
            sent[g].at[me], st[g].at[pl.ds(2 * me, CAP)], own_s.at[g]
        )
        copy.start()

    def passages(g):
        for dz, dx in STEPS:
            other = around(z, dz) * SIDE + around(x_, dx)
            to = st[g].at[pl.ds(2 * me, CAP)]
            remote(sent[g].at[other], to, st_s.at[g], st_r.at[g], (sec, other)).start()

    def passages_wait(g):
        pltpu.make_async_copy(
            sent[g].at[me], st[g].at[pl.ds(2 * me, CAP)], own_s.at[g]
        ).wait()
        arrived(st[g].at[pl.ds(0, CAP * (N_DEV - 1))], st_s.at[g], st_r.at[g])

    for half in range(2):
        src = chunk(half, 2, 0)
        ag_wait(half, src, 2)
        ag(half, src, whole, 12, ahead[1 - half][0])
        ag(half, src, whole, 13, ahead[1 - half][1])

    def second_axis(k, first):
        b = 3 + 3 * k
        for half in range(2):
            src = chunk(half, first, -1)
            ag_wait(half, src, b)
            ag(half, src, top, b + 2, ahead[1 - half][0])
            src = chunk(half, first, 1)
            ag_wait(half, src, b + 1)
            ag(half, src, bottom, b + 2, ahead[1 - half][1])

    second_axis(0, 0)

    for half in range(2):
        p, c = parts[half], spot[half]
        rs_arrived(half, l1.at[half], 0)
        block = p.at[around(c, 1), lo]
        block[...] = (block[...].astype(F32) + l1[half].astype(F32)).astype(BF16)
        rs(half, block, l2.at[half, lo], 2, ahead[half][0])
        rs_arrived(half, r1.at[half], 1)
        block = p.at[around(c, -1), hi]
        block[...] = (block[...].astype(F32) + r1[half].astype(F32)).astype(BF16)
        rs(half, block, r2.at[half, hi], 3, ahead[half][1])

    second_axis(1, -1)
    second_axis(2, 1)
    second_axis(3, 2)

    for half in range(2):
        p, c = parts[half], spot[half]
        rs_arrived(half, l2.at[half], 2)
        rs_arrived(half, r2.at[half], 3)
        for u in range(SIDE):
            block = p.at[c, u]
            total = block[...].astype(F32) + l2[half, u].astype(F32) + r2[half, u].astype(F32)
            block[...] = total.astype(BF16)
        for k in (1, 3, 2):
            other = around(spot[1 - half], k)
            target = at(other, x_) if half == 0 else at(z, other)
            rs(half, p.at[c, other], z2.at[half, k - 1], 4, target)
    passages(0)

    for k in (6, 7, 8):
        loads[k].wait()
    for half in range(2):
        for k in range(SIDE):
            ag_wait(half, chunk(half, (0, -1, 1, 2)[k], 2), 5 + 3 * k)

    def project_queries(k):
        span = pl.ds(pl.multiple_of(k * 2 * QLEN, 2 * QLEN), 2 * QLEN)
        weight = qv[span, :]
        for half in range(2):
            qacc[half] += jnp.dot(xall[half, k], weight, preferred_element_type=F32)

    qacc[...] = jnp.zeros_like(qacc)
    loop(N_DEV, project_queries)
    token_at = lax.broadcasted_iota(jnp.int32, (QLEN, 1), 0) + TOPK * PASS_LEN
    token_angles = token_at.astype(F32) * frequency
    cosine, sine = lane_tables(token_angles)
    base = 2 * mine
    for half in range(2):
        for j in range(2):
            head = turned(qacc[half, :, j * HD : (j + 1) * HD], cosine, sine)
            q4[half, base + j] = head.astype(BF16)
        block = q4.at[half, pl.ds(base, 2)]
        push(sends, block, block, q_s.at[half], q_r.at[half], pair)

    for g in range(1, GROUPS):
        passages(g)

    slot_at = lax.broadcasted_iota(jnp.int32, (SLOTS, 1), 0)
    offsets = jnp.zeros((SLOTS, 1), jnp.int32)
    for j in range(SLOTS):
        offsets = jnp.where(slot_at == j, order[0, j // TOPK, j % TOPK] * PASS_LEN, offsets)
    places = rec[0] + offsets
    angle[pl.ds(0, QLEN)] = token_angles
    for i in range(FRESH):
        here = places[:, i : i + 1]
        if FRESH + i < RECOMP:
            here = jnp.where(mine == 0, here, places[:, FRESH + i : FRESH + i + 1])
        angle[pl.ds(QLEN + i * SLOTS, SLOTS)] = here.astype(F32) * frequency
    cosine, sine = lane_tables(angle[...])
    for half in range(2):
        p, c = parts[half], spot[half]
        total = p[c, spot[1 - half]].astype(F32)
        rs_arrived(half, z2.at[half], 4)
        for k in range(1, SIDE):
            total += z2[half, k - 1].astype(F32)
        total = total.astype(BF16).astype(F32)
        if half == 0:
            total = turned(total, cosine, sine)
        own_to, fresh_to = (ko, kf) if half == 0 else (vo, vf)
        own_to[...] = total[:QLEN].astype(BF16)
        fresh = total[QLEN:].reshape(FRESH, SLOTS, HD)
        for r in range(REQ_SECTION):
            rows_of = fresh[:, r * TOPK : (r + 1) * TOPK].reshape(FRESH * TOPK, HD)
            filler = jnp.zeros((FROWS - FRESH * TOPK, HD), F32)
            fresh_to[r] = jnp.concatenate([rows_of, filler], axis=0).astype(BF16)

    cols = 4 * QLEN

    def score(keys, queries):
        s = lax.dot_general(
            keys, queries, (((1,), (1,)), ((), ())), preferred_element_type=F32
        )
        return s * SCALE

    def update(r, scores, values):
        old = m[r]
        new = old
        for s in scores:
            new = jnp.maximum(new, jnp.max(s, axis=0, keepdims=True))
        scale = jnp.exp2(old - new)
        total, mixed = l[r] * scale, acc[r] * scale
        for s, v in zip(scores, values):
            weights = jnp.exp2(s - new)
            total = total + jnp.sum(weights, axis=0, keepdims=True)
            mixed = mixed + lax.dot_general(
                v, weights.astype(BF16), (((0,), (0,)), ((), ())), preferred_element_type=F32
            )
        m[r], l[r], acc[r] = new, total, mixed

    def bias(count, valid):
        index = lax.broadcasted_iota(jnp.int32, (count, 1), 0)
        return jnp.where(index < valid, 0.0, -jnp.inf)

    def queries_of(r):
        return q4[r].reshape(cols, HD)

    def stored(r, g):
        many = 2 if g == 0 else 4

        def some(k):
            scores, values = [], []
            for i in range(many):
                e = ent[r * TOPK + many * k + i]
                block = st[g].at[e]
                s = score(block[:, :HD], queries_of(r))
                if g == GROUPS - 1:
                    s = s + bias(PIECES[g], PIECES[g] - (2 * HALF - KEPT) * mine)
                scores.append(s)
                values.append(block[:, HD:])
            update(r, scores, values)

        loop(TOPK // many, some)

    for half in range(2):
        block = q4.at[half, pl.ds(2 - base, 2)]
        arrived(block, q_s.at[half], q_r.at[half])
    m[...] = jnp.full_like(m, -1e30)
    l[...] = jnp.zeros_like(l)
    acc[...] = jnp.zeros_like(acc)
    for r in range(REQ_SECTION):
        s = score(kf[r], queries_of(r)) + bias(FROWS, FRESH * TOPK - TOPK * mine)
        update(r, [s], [vf[r]])
    s = score(ko[...], queries_of(mine))
    keys_at = lax.broadcasted_iota(jnp.int32, (QLEN, cols), 0)
    query_at = lax.rem(lax.broadcasted_iota(jnp.int32, (QLEN, cols), 1), QLEN)
    s = jnp.where(keys_at <= query_at, s, -jnp.inf)
    update(mine, [s], [vo[...]])

    def finish(r):
        done = (acc[r] / l[r]).astype(BF16)
        level = m[r] + jnp.log2(l[r])
        for j in range(4):
            span = slice(j * QLEN, (j + 1) * QLEN)
            oall[r, j // 2, pl.ds((j % 2) * HD, HD), :] = done[:, span]
            lall[r, j // 2, pl.ds(j % 2, 1), :] = level[:, span]
        push(sends, oall.at[r, 1 - mine], oin.at[r], ex_s.at[2 * r], ex_r.at[2 * r], pair)
        push(sends, lall.at[r, 1 - mine], lin.at[r], ex_s.at[2 * r + 1], ex_r.at[2 * r + 1], pair)

    def join(r):
        arrived(oin.at[r], ex_s.at[2 * r], ex_r.at[2 * r])
        arrived(lin.at[r], ex_s.at[2 * r + 1], ex_r.at[2 * r + 1])
        for j in range(2):
            a, b = lall[r, mine, pl.ds(j, 1), :], lin[r, pl.ds(j, 1), :]
            most = jnp.maximum(a, b)
            a, b = jnp.exp2(a - most), jnp.exp2(b - most)
            span = pl.ds(j * HD, HD)
            joined = oall[r, mine, span, :].astype(F32) * a + oin[r, span, :].astype(F32) * b
            joined = joined / (a + b)
            att[r * QLEN : (r + 1) * QLEN, j * HD : (j + 1) * HD] = joined.T.astype(BF16)

    size = REQ_SECTION * QLEN // BLOCKS
    part = size // 2
    width = xall.shape[3]

    def units(b, half, first, second, count):
        return xall.at[half, pl.ds(first * SIDE + second, count), pl.ds(b * part, part)]

    def compute(b, xx, zz):
        span = pl.ds(pl.multiple_of((zz * SIDE + xx) * width, width), width)
        got = jnp.dot(
            att[b * size : (b + 1) * size, :], wv[:, span], preferred_element_type=F32
        ).astype(BF16)
        xall[0, xx * SIDE + zz, pl.ds(b * part, part)] = got[:part]
        xall[1, zz * SIDE + xx, pl.ds(b * part, part)] = got[part:]

    def out_push(b, half, sem, src, dst, target):
        s = 2 * b + half
        remote(src, dst, br_s.at[s], br_r.at[5 * s + sem], target).start()

    def out_arrived(b, half, sem, block):
        s = 2 * b + half
        arrived(block, br_s.at[s], br_r.at[5 * s + sem])

    def first(b):
        loop(SIDE, lambda k: compute(b, around(x_, 2), around(z, k)))
        loop(SIDE - 1, lambda k: compute(b, around(x_, skip_two(k)), around(z, 2)))
        for half in range(2):
            c = spot[half]
            out_push(b, half, 0, units(b, half, around(c, 2), 0, 2), bl1.at[b, half], ahead[half][0])
            out_push(b, half, 1, units(b, half, around(c, 2), 2, 2), br1.at[b, half], ahead[half][1])
        loop(
            9,
            lambda k: compute(
                b, around(x_, skip_two(k // 3)), around(z, skip_two(lax.rem(k, 3)))
            ),
        )
        for half in range(2):
            c = spot[half]
            out_push(b, half, 2, units(b, half, around(c, 1), 2, 2), bl2.at[b, half, hi], ahead[half][0])
            out_push(b, half, 3, units(b, half, around(c, -1), 0, 2), br2.at[b, half, lo], ahead[half][1])

    def second(b):
        for half in range(2):
            c = spot[half]
            out_arrived(b, half, 0, bl1.at[b, half])
            block = units(b, half, around(c, 1), 0, 2)
            block[...] = (block[...].astype(F32) + bl1[b, half].astype(F32)).astype(BF16)
            out_push(b, half, 2, block, bl2.at[b, half, lo], ahead[half][0])
            out_arrived(b, half, 1, br1.at[b, half])
            block = units(b, half, around(c, -1), 2, 2)
            block[...] = (block[...].astype(F32) + br1[b, half].astype(F32)).astype(BF16)
            out_push(b, half, 3, block, br2.at[b, half, hi], ahead[half][1])

    def third(b):
        for half in range(2):
            c = spot[half]
            out_arrived(b, half, 2, bl2.at[b, half])
            out_arrived(b, half, 3, br2.at[b, half])
            block = units(b, half, c, 0, SIDE)
            total = block[...].astype(F32) + bl2[b, half].astype(F32) + br2[b, half].astype(F32)
            block[...] = total.astype(BF16)
            for k in (1, 3, 2, 0):
                other = around(spot[1 - half], k)
                target = (after, other * SIDE + x_) if half == 0 else (after, z * SIDE + other)
                src = xall.at[half, c * SIDE + other, pl.ds(b * part, part)]
                out_push(b, half, 4, src, bz2.at[b, half, k], target)

    results = []

    def fourth(b):
        if b > 1:
            results[b - 2].wait()
        for half in range(2):
            out_arrived(b, half, 4, bz2.at[b, half])
            total = bz2[b, half, 0].astype(F32)
            for k in range(1, SIDE):
                total += bz2[b, half, k].astype(F32)
            outv[b % 2, pl.ds(half * part, part), :] = total
        to = out.at[pl.ds(b * size, size)]
        results.append(pltpu.make_async_copy(outv.at[b % 2], to, loc.at[10 + b]))
        results[b].start()

    for g in range(GROUPS - 1):
        passages_wait(g)
        stored(0, g)
        stored(1, g)
    for half in range(2):
        gone = xall.at[half, pl.ds(0, N_DEV - 1)]
        remote(gone, gone, ag_s.at[half], ag_r.at[0], right).wait_send()
    loads[9].wait()
    passages_wait(GROUPS - 1)
    stored(0, GROUPS - 1)
    finish(0)
    stored(1, GROUPS - 1)
    finish(1)
    join(0)
    per = BLOCKS // REQ_SECTION
    for b in range(per):
        first(b)
    join(1)
    for b in range(BLOCKS):
        if per + b < BLOCKS:
            first(per + b)
        second(b)
        if b > 0:
            third(b - 1)
    third(BLOCKS - 1)
    for b in range(BLOCKS):
        fourth(b)
    for copy in sends:
        copy.wait_send()

    def gone(block, sem):
        remote(block, block, sem, br_r.at[0], right).wait_send()

    for half in range(2):
        gone(parts[half].at[pl.ds(0, SIDE - 1)], rs_s.at[2 * half])
        gone(parts[half].at[0, pl.ds(0, SIDE - 1)], rs_s.at[2 * half + 1])
        for b in range(BLOCKS):
            gone(units(b, half, 0, 0, N_DEV), br_s.at[2 * b + half])
    for g in range(GROUPS):
        gone(sent[g].at[pl.ds(0, N_DEV - 1)], st_s.at[g])
    for copy in results[-2:]:
        copy.wait()


def layer(home, retrieved, order, x, hid, kvw, qw, ow, store, rec, freq):
    anywhere = pl.BlockSpec(memory_space=pl.ANY)
    vmem = pl.BlockSpec(memory_space=pltpu.VMEM)
    smem = pl.BlockSpec(memory_space=pltpu.SMEM)
    dma = pltpu.SemaphoreType.DMA
    d_here = x.shape[1]
    cols = 4 * QLEN
    part = REQ_SECTION * QLEN // BLOCKS // 2
    width = ow.shape[1] // N_DEV
    assert width == d_here

    def bf16(*shape):
        return pltpu.VMEM(shape, BF16)

    def f32(*shape):
        return pltpu.VMEM(shape, F32)

    return pl.pallas_call(
        layer_kernel,
        out_shape=jax.ShapeDtypeStruct((REQ_SECTION * QLEN, width), F32),
        in_specs=[smem] * 3 + [anywhere] * 6 + [vmem] * 2,
        out_specs=anywhere,
        scratch_shapes=[
            pltpu.SMEM((SLOTS,), jnp.int32),
            bf16(2, N_DEV, QLEN, d_here),
            bf16(*qw.shape),
            bf16(*kvw.shape),
            bf16(REQ_SECTION, GROUP, d_here),
            bf16(SIDE, SIDE, GROUP, HD),
            bf16(SIDE, SIDE, GROUP, HD),
            bf16(2, 2, GROUP, HD),
            bf16(2, 2, GROUP, HD),
            bf16(2, SIDE, GROUP, HD),
            bf16(2, SIDE, GROUP, HD),
            bf16(2, SIDE - 1, GROUP, HD),
            f32(2, QLEN, 2 * HD),
            bf16(*store.shape),
            *[bf16(N_DEV, CAP, piece, 2 * HD) for piece in PIECES],
            *[bf16(N_DEV * CAP, piece, 2 * HD) for piece in PIECES],
            bf16(REQ_SECTION, 4, QLEN, HD),
            bf16(REQ_SECTION, FROWS, HD),
            bf16(REQ_SECTION, FROWS, HD),
            bf16(QLEN, HD),
            bf16(QLEN, HD),
            f32(REQ_SECTION, HD, cols),
            f32(REQ_SECTION, 1, cols),
            f32(REQ_SECTION, 1, cols),
            f32(GROUP, HD),
            bf16(REQ_SECTION, 2, 2 * HD, QLEN),
            f32(REQ_SECTION, 2, 8, QLEN),
            bf16(REQ_SECTION, 2 * HD, QLEN),
            f32(REQ_SECTION, 8, QLEN),
            bf16(*ow.shape),
            bf16(REQ_SECTION * QLEN, 2 * HD),
            bf16(BLOCKS, 2, 2, part, width),
            bf16(BLOCKS, 2, 2, part, width),
            bf16(BLOCKS, 2, SIDE, part, width),
            bf16(BLOCKS, 2, SIDE, part, width),
            bf16(BLOCKS, 2, SIDE, part, width),
            f32(2, 2 * part, width),
            dma((10 + BLOCKS,)),
            dma((GROUPS,)),
            dma((2,)),
            dma((30,)),
            dma((4,)),
            dma((10,)),
            dma((GROUPS,)),
            dma((GROUPS,)),
            dma((2,)),
            dma((2,)),
            dma((4,)),
            dma((4,)),
            dma((2 * BLOCKS,)),
            dma((10 * BLOCKS,)),
        ],
        compiler_params=pltpu.CompilerParams(
            collective_id=0, has_side_effects=True, vmem_limit_bytes=63 * 2**20
        ),
        name="layer",
    )(home, retrieved, order, x, hid, kvw, qw, ow, store, rec, freq)


def body(
    activations, q_weight, out_weight, kv_weight, passage_store,
    passage_home, retrieved, slot_order, recomputed, passage_hidden,
):
    exponents = -np.arange(HD // 2, dtype=np.float32) * np.float32(2.0 / HD)
    frequency = np.float32(ROPE_BASE) ** exponents
    frequency = jnp.asarray(np.concatenate([frequency, frequency])[None])
    hidden = passage_hidden[0].transpose(1, 0, 2).reshape(RECOMP * SLOTS, -1)
    out = layer(
        passage_home, retrieved, slot_order, activations[0], hidden, kv_weight[0], q_weight[0],
        out_weight[0], passage_store[0], recomputed, frequency,
    )
    return out.astype(BF16)[None]


def solution(mesh):
    in_specs = (
        P("section", None, "dev"),
        P("section", None, "dev"),
        P("section", "dev", None),
        P("section", "dev", None),
        P("section", "dev", None, None, None),
        P("section", None),
        P("section", None, None),
        P("section", None, None),
        P("section", None, None),
        P("section", None, None, "dev"),
    )
    out_specs = P("section", None, "dev")
    return jax.shard_map(body, mesh=mesh, in_specs=in_specs, out_specs=out_specs, check_vma=False)
```

time: 221 us -> 201 us (0.910)
  Pallas kernels: 215 us -> 199 us
  local copies, waits for them, and re-layouts: 3.12 us -> 0 us
    pallas_call x1, Pallas kernels: 215 us -> 199 us  [layer(): pl.pallas_call(layer_kernel, out_shape=jax.ShapeDtypeStruct((REQ_SECTION...]
where the time goes in v3:
time: 201 us
  Pallas kernels  199 us (99%)
  other arithmetic  2.08 us (1%)
    pallas_call x1, Pallas kernels, layer(): pl.pallas_call(layer_kernel, out_shape=jax.ShapeDtypeStruct((REQ_SECTION...  199 us

profile of v3, /device:TPU:15, one launch (start us, length us, event | category | flops | bytes accessed | tf_op | source)
XLA Modules:
  0.0 200.9 jit_solution(9195626535275503219)
XLA Ops:
  0.0 198.8 %layer.1 = f32[512,512]{1,0:T(8,128)} custom-call(s32[1,64]{1,0:T(1,128)} %home.1, s32[1,2,8]{2,1,0:T(2,128)} %retrieved.1, s32[1,2,8]{2,1,0:T(2,128)} %order.1, bf16[512,512]{1,0:T(8,128)(2,1)} %bitcast.17, bf16[1232,512]{1,0:T(8,128)(2,1)} %bitcast.16, bf16[512,2048]{1,0:T(8,128)(2,1)} %bitcast.15, bf16[8192,256]{1,0:T(8,128)(2,1)} %bitcast.13, ...), custom_call_target="tpu_custom_call" | custom-call | tf_op jit(solution)/shard_map/layer/pallas_call | solution.py:610
  198.8 2.1 %convert_bitcast_fusion = bf16[1,512,512]{2,1,0:T(8,128)(2,1)} fusion(f32[512,512]{1,0:T(8,128)} %layer.1), kind=kLoop, calls=%fused_computation | loop fusion | flops 262144 | bytes 1572864 | tf_op jit(solution)/shard_map/broadcast_in_dim | solution.py:687

commit v4 on v3

--- a/solution.py
+++ b/solution.py
@@ -26,10 +26,11 @@
 FROWS = 320
 KEPT = PASS_LEN - RECOMP
 HALF = 224
-PIECES = (112, 64, 48)
-STARTS = (0, 112, 176)
+PIECES = (128, 64, 32)
+STARTS = (0, 128, 192)
 GROUPS = len(PIECES)
 BLOCKS = 4
+FIRSTS = ((0,), (1,))
 ROPE_BASE = 500000.0
 MESH = pl.DeviceIdType.MESH
 F32 = jnp.float32
@@ -67,14 +68,14 @@
 
 
 STEPS = (
-    (0, 1), (0, 3), (1, 0), (3, 0), (1, 1), (3, 3), (1, 3), (3, 1),
-    (0, 2), (2, 0), (2, 1), (2, 3), (1, 2), (3, 2), (2, 2),
+    (1, 1), (3, 3), (0, 2), (1, 3), (3, 1), (2, 0), (2, 1), (0, 3),
+    (3, 2), (1, 0), (2, 3), (0, 1), (1, 2), (3, 0), (2, 2),
 )
 
 
 def layer_kernel(
     home, retrieved, order, x, hid, kvw, qw, ow, store, rec, freq, out,
-    ent, xall, qv, kvv, rows, pa, pb, l1, r1, l2, r2, z2, qacc,
+    ent, xall, qv, kvv, rows, pa, pb, l1, r1, l2, r2, z1, z2, qacc,
     storev, out0, out1, out2, st0, st1, st2, q4, kf, vf, ko, vo, acc, m, l,
     angle, oall, lall, oin, lin, wv, att, bl1, br1, bl2, br2, bz2, outv,
     loc, own_s, ag_s, ag_r, rs_s, rs_r, st_s, st_r, q_s, q_r, ex_s, ex_r, br_s, br_r,
@@ -183,10 +184,12 @@
     lo, hi = pl.ds(0, 2), pl.ds(2, 2)
 
     def rs(half, src, dst, sem, target):
-        remote(src, dst, rs_s.at[2 * half + sem // 4], rs_r.at[5 * half + sem], target).start()
+        remote(src, dst, rs_s.at[2 * half + sem // 4], rs_r.at[8 * half + sem], target).start()
 
     def rs_arrived(half, block, sem):
-        arrived(block, rs_s.at[2 * half + sem // 4], rs_r.at[5 * half + sem])
+        arrived(block, rs_s.at[2 * half + sem // 4], rs_r.at[8 * half + sem])
+
+    upper, lower = pl.ds(0, GROUP // 32 * 16), pl.ds(GROUP // 32 * 16, GROUP - GROUP // 32 * 16)
 
     def rs_first(half):
         p, c = parts[half], spot[half]
@@ -317,10 +320,17 @@
             block = p.at[c, u]
             total = block[...].astype(F32) + l2[half, u].astype(F32) + r2[half, u].astype(F32)
             block[...] = total.astype(BF16)
-        for k in (1, 3, 2):
-            other = around(spot[1 - half], k)
-            target = at(other, x_) if half == 0 else at(z, other)
-            rs(half, p.at[c, other], z2.at[half, k - 1], 4, target)
+        far = around(spot[1 - half], 2)
+        rs(half, p.at[c, far, upper], z1.at[half, upper], 4, ahead[1 - half][0])
+        rs(half, p.at[c, far, lower], z1.at[half, lower], 5, ahead[1 - half][1])
+    for half in range(2):
+        p, c, d = parts[half], spot[half], spot[1 - half]
+        for k, span in ((1, upper), (-1, lower)):
+            rs_arrived(half, z1.at[half, span], 4 + (1 - k) // 2)
+            block = p.at[c, around(d, k), span]
+            block[...] = (block[...].astype(F32) + z1[half, span].astype(F32)).astype(BF16)
+        rs(half, p.at[c, around(d, 1)], z2.at[half, 0], 6, ahead[1 - half][0])
+        rs(half, p.at[c, around(d, -1)], z2.at[half, 1], 7, ahead[1 - half][1])
     passages(0)
 
     for k in (6, 7, 8):
@@ -345,11 +355,16 @@
         for j in range(2):
             head = turned(qacc[half, :, j * HD : (j + 1) * HD], cosine, sine)
             q4[half, base + j] = head.astype(BF16)
-        block = q4.at[half, pl.ds(base, 2)]
-        push(sends, block, block, q_s.at[half], q_r.at[half], pair)
+
+    def share_queries(r):
+        block = q4.at[r, pl.ds(base, 2)]
+        push(sends, block, block, q_s.at[r], q_r.at[r], pair)
+
+    share_queries(0)
 
     for g in range(1, GROUPS):
         passages(g)
+    share_queries(1)
 
     slot_at = lax.broadcasted_iota(jnp.int32, (SLOTS, 1), 0)
     offsets = jnp.zeros((SLOTS, 1), jnp.int32)
@@ -366,9 +381,9 @@
     for half in range(2):
         p, c = parts[half], spot[half]
         total = p[c, spot[1 - half]].astype(F32)
-        rs_arrived(half, z2.at[half], 4)
-        for k in range(1, SIDE):
-            total += z2[half, k - 1].astype(F32)
+        for k in range(2):
+            rs_arrived(half, z2.at[half, k], 6 + k)
+            total += z2[half, k].astype(F32)
         total = total.astype(BF16).astype(F32)
         if half == 0:
             total = turned(total, cosine, sine)
@@ -427,20 +442,26 @@
 
         loop(TOPK // many, some)
 
-    for half in range(2):
-        block = q4.at[half, pl.ds(2 - base, 2)]
-        arrived(block, q_s.at[half], q_r.at[half])
+    def computed(r):
+        block = q4.at[r, pl.ds(2 - base, 2)]
+        arrived(block, q_s.at[r], q_r.at[r])
+        s = score(kf[r], queries_of(r)) + bias(FROWS, FRESH * TOPK - TOPK * mine)
+        update(r, [s], [vf[r]])
+
+        @pl.when(mine == r)
+        def _():
+            s = score(ko[...], queries_of(r))
+            keys_at = lax.broadcasted_iota(jnp.int32, (QLEN, cols), 0)
+            query_at = lax.rem(lax.broadcasted_iota(jnp.int32, (QLEN, cols), 1), QLEN)
+            s = jnp.where(keys_at <= query_at, s, -jnp.inf)
+            update(r, [s], [vo[...]])
+
     m[...] = jnp.full_like(m, -1e30)
     l[...] = jnp.zeros_like(l)
     acc[...] = jnp.zeros_like(acc)
-    for r in range(REQ_SECTION):
-        s = score(kf[r], queries_of(r)) + bias(FROWS, FRESH * TOPK - TOPK * mine)
-        update(r, [s], [vf[r]])
-    s = score(ko[...], queries_of(mine))
-    keys_at = lax.broadcasted_iota(jnp.int32, (QLEN, cols), 0)
-    query_at = lax.rem(lax.broadcasted_iota(jnp.int32, (QLEN, cols), 1), QLEN)
-    s = jnp.where(keys_at <= query_at, s, -jnp.inf)
-    update(mine, [s], [vo[...]])
+    per = BLOCKS // REQ_SECTION
+
+    size = REQ_SECTION * QLEN // BLOCKS
 
     def finish(r):
         done = (acc[r] / l[r]).astype(BF16)
@@ -449,35 +470,45 @@
             span = slice(j * QLEN, (j + 1) * QLEN)
             oall[r, j // 2, pl.ds((j % 2) * HD, HD), :] = done[:, span]
             lall[r, j // 2, pl.ds(j % 2, 1), :] = level[:, span]
-        push(sends, oall.at[r, 1 - mine], oin.at[r], ex_s.at[2 * r], ex_r.at[2 * r], pair)
-        push(sends, lall.at[r, 1 - mine], lin.at[r], ex_s.at[2 * r + 1], ex_r.at[2 * r + 1], pair)
-
-    def join(r):
-        arrived(oin.at[r], ex_s.at[2 * r], ex_r.at[2 * r])
-        arrived(lin.at[r], ex_s.at[2 * r + 1], ex_r.at[2 * r + 1])
+        sem = (1 + per) * r
+        push(sends, lall.at[r, 1 - mine], lin.at[r], ex_s.at[sem], ex_r.at[sem], pair)
+        for k in range(per):
+            span = pl.ds(k * size, size)
+            push(sends, oall.at[r, 1 - mine, :, span], oin.at[r, :, span],
+                 ex_s.at[sem + 1 + k], ex_r.at[sem + 1 + k], pair)
+
+    def join(b):
+        r, k = b // per, b % per
+        sem = (1 + per) * r
+        if k == 0:
+            arrived(lin.at[r], ex_s.at[sem], ex_r.at[sem])
+        here = pl.ds(k * size, size)
+        arrived(oin.at[r, :, here], ex_s.at[sem + 1 + k], ex_r.at[sem + 1 + k])
         for j in range(2):
-            a, b = lall[r, mine, pl.ds(j, 1), :], lin[r, pl.ds(j, 1), :]
-            most = jnp.maximum(a, b)
-            a, b = jnp.exp2(a - most), jnp.exp2(b - most)
+            a, b_ = lall[r, mine, pl.ds(j, 1), here], lin[r, pl.ds(j, 1), here]
+            most = jnp.maximum(a, b_)
+            a, b_ = jnp.exp2(a - most), jnp.exp2(b_ - most)
             span = pl.ds(j * HD, HD)
-            joined = oall[r, mine, span, :].astype(F32) * a + oin[r, span, :].astype(F32) * b
-            joined = joined / (a + b)
-            att[r * QLEN : (r + 1) * QLEN, j * HD : (j + 1) * HD] = joined.T.astype(BF16)
-
-    size = REQ_SECTION * QLEN // BLOCKS
+            joined = oall[r, mine, span, here].astype(F32) * a
+            joined = (joined + oin[r, span, here].astype(F32) * b_) / (a + b_)
+            att[b * size : (b + 1) * size, j * HD : (j + 1) * HD] = joined.T.astype(BF16)
+
     part = size // 2
     width = xall.shape[3]
 
     def units(b, half, first, second, count):
         return xall.at[half, pl.ds(first * SIDE + second, count), pl.ds(b * part, part)]
 
-    def compute(b, xx, zz):
+    def compute(blocks, xx, zz):
         span = pl.ds(pl.multiple_of((zz * SIDE + xx) * width, width), width)
+        from_row, to_row = blocks[0] * size, (blocks[-1] + 1) * size
         got = jnp.dot(
-            att[b * size : (b + 1) * size, :], wv[:, span], preferred_element_type=F32
+            att[from_row:to_row, :], wv[:, span], preferred_element_type=F32
         ).astype(BF16)
-        xall[0, xx * SIDE + zz, pl.ds(b * part, part)] = got[:part]
-        xall[1, zz * SIDE + xx, pl.ds(b * part, part)] = got[part:]
+        for k, b in enumerate(blocks):
+            here = pl.ds(b * part, part)
+            xall[0, xx * SIDE + zz, here] = got[k * size : k * size + part]
+            xall[1, zz * SIDE + xx, here] = got[k * size + part : (k + 1) * size]
 
     def out_push(b, half, sem, src, dst, target):
         s = 2 * b + half
@@ -487,23 +518,25 @@
         s = 2 * b + half
         arrived(block, br_s.at[s], br_r.at[5 * s + sem])
 
-    def first(b):
-        loop(SIDE, lambda k: compute(b, around(x_, 2), around(z, k)))
-        loop(SIDE - 1, lambda k: compute(b, around(x_, skip_two(k)), around(z, 2)))
-        for half in range(2):
-            c = spot[half]
-            out_push(b, half, 0, units(b, half, around(c, 2), 0, 2), bl1.at[b, half], ahead[half][0])
-            out_push(b, half, 1, units(b, half, around(c, 2), 2, 2), br1.at[b, half], ahead[half][1])
+    def first(blocks):
+        loop(SIDE, lambda k: compute(blocks, around(x_, 2), around(z, k)))
+        loop(SIDE - 1, lambda k: compute(blocks, around(x_, skip_two(k)), around(z, 2)))
+        for b in blocks:
+            for half in range(2):
+                c, to, back = spot[half], *ahead[half]
+                out_push(b, half, 0, units(b, half, around(c, 2), 0, 2), bl1.at[b, half], to)
+                out_push(b, half, 1, units(b, half, around(c, 2), 2, 2), br1.at[b, half], back)
         loop(
             9,
             lambda k: compute(
-                b, around(x_, skip_two(k // 3)), around(z, skip_two(lax.rem(k, 3)))
+                blocks, around(x_, skip_two(k // 3)), around(z, skip_two(lax.rem(k, 3)))
             ),
         )
-        for half in range(2):
-            c = spot[half]
-            out_push(b, half, 2, units(b, half, around(c, 1), 2, 2), bl2.at[b, half, hi], ahead[half][0])
-            out_push(b, half, 3, units(b, half, around(c, -1), 0, 2), br2.at[b, half, lo], ahead[half][1])
+        for b in blocks:
+            for half in range(2):
+                c, to, back = spot[half], *ahead[half]
+                out_push(b, half, 2, units(b, half, around(c, 1), 2, 2), bl2.at[b, half, hi], to)
+                out_push(b, half, 3, units(b, half, around(c, -1), 0, 2), br2.at[b, half, lo], back)
 
     def second(b):
         for half in range(2):
@@ -546,31 +579,36 @@
         results.append(pltpu.make_async_copy(outv.at[b % 2], to, loc.at[10 + b]))
         results[b].start()
 
-    for g in range(GROUPS - 1):
+    computed(0)
+    for g in range(GROUPS):
         passages_wait(g)
         stored(0, g)
-        stored(1, g)
+    finish(0)
     for half in range(2):
         gone = xall.at[half, pl.ds(0, N_DEV - 1)]
         remote(gone, gone, ag_s.at[half], ag_r.at[0], right).wait_send()
     loads[9].wait()
-    passages_wait(GROUPS - 1)
-    stored(0, GROUPS - 1)
-    finish(0)
-    stored(1, GROUPS - 1)
+    for group in FIRSTS:
+        for b in group:
+            join(b)
+        first(group)
+    computed(1)
+    stored(1, 0)
+    second(0)
+    second(1)
+    for g in range(1, GROUPS):
+        stored(1, g)
     finish(1)
-    join(0)
-    per = BLOCKS // REQ_SECTION
-    for b in range(per):
-        first(b)
-    join(1)
-    for b in range(BLOCKS):
-        if per + b < BLOCKS:
-            first(per + b)
-        second(b)
-        if b > 0:
-            third(b - 1)
-    third(BLOCKS - 1)
+    third(0)
+    join(2)
+    first((2,))
+    third(1)
+    join(3)
+    first((3,))
+    second(2)
+    second(3)
+    third(2)
+    third(3)
     for b in range(BLOCKS):
         fourth(b)
     for copy in sends:
@@ -624,7 +662,8 @@
             bf16(2, 2, GROUP, HD),
             bf16(2, SIDE, GROUP, HD),
             bf16(2, SIDE, GROUP, HD),
-            bf16(2, SIDE - 1, GROUP, HD),
+            bf16(2, GROUP, HD),
+            bf16(2, 2, GROUP, HD),
             f32(2, QLEN, 2 * HD),
             bf16(*store.shape),
             *[bf16(N_DEV, CAP, piece, 2 * HD) for piece in PIECES],
@@ -655,13 +694,13 @@
             dma((2,)),
             dma((30,)),
             dma((4,)),
-            dma((10,)),
+            dma((16,)),
             dma((GROUPS,)),
             dma((GROUPS,)),
             dma((2,)),
             dma((2,)),
-            dma((4,)),
-            dma((4,)),
+            dma((2 + BLOCKS,)),
+            dma((2 + BLOCKS,)),
             dma((2 * BLOCKS,)),
             dma((10 * BLOCKS,)),
         ],

time: 201 us -> 197 us (0.980)
  Pallas kernels: 199 us -> 193 us
    pallas_call x1, Pallas kernels: 199 us -> 193 us  [layer(): pl.pallas_call(layer_kernel, out_shape=jax.ShapeDtypeStruct((REQ_SECTION...]
where the time goes in v4:
time: 197 us; the launch traced here: 195 us
  Pallas kernels  193 us (98%)
  other arithmetic  2.08 us (1%)
    pallas_call x1, Pallas kernels, layer(): pl.pallas_call(layer_kernel, out_shape=jax.ShapeDtypeStruct((REQ_SECTION...  193 us

profile of v4, /device:TPU:15, one launch (start us, length us, event | category | flops | bytes accessed | tf_op | source)
XLA Modules:
  0.0 194.9 jit_solution(10505162530233943571)
XLA Ops:
  0.0 192.8 %layer.1 = f32[512,512]{1,0:T(8,128)} custom-call(s32[1,64]{1,0:T(1,128)} %home.1, s32[1,2,8]{2,1,0:T(2,128)} %retrieved.1, s32[1,2,8]{2,1,0:T(2,128)} %order.1, bf16[512,512]{1,0:T(8,128)(2,1)} %bitcast.17, bf16[1232,512]{1,0:T(8,128)(2,1)} %bitcast.16, bf16[512,2048]{1,0:T(8,128)(2,1)} %bitcast.15, bf16[8192,256]{1,0:T(8,128)(2,1)} %bitcast.13, ...), custom_call_target="tpu_custom_call" | custom-call | tf_op jit(solution)/shard_map/layer/pallas_call | solution.py:648
  192.8 2.1 %convert_bitcast_fusion = bf16[1,512,512]{2,1,0:T(8,128)(2,1)} fusion(f32[512,512]{1,0:T(8,128)} %layer.1), kind=kLoop, calls=%fused_computation | loop fusion | flops 262144 | bytes 1572864 | tf_op jit(solution)/shard_map/broadcast_in_dim | solution.py:726

commit v5 on v4

--- a/solution.py
+++ b/solution.py
@@ -78,7 +78,7 @@
     ent, xall, qv, kvv, rows, pa, pb, l1, r1, l2, r2, z1, z2, qacc,
     storev, out0, out1, out2, st0, st1, st2, q4, kf, vf, ko, vo, acc, m, l,
     angle, oall, lall, oin, lin, wv, att, bl1, br1, bl2, br2, bz2, outv,
-    loc, own_s, ag_s, ag_r, rs_s, rs_r, st_s, st_r, q_s, q_r, ex_s, ex_r, br_s, br_r,
+    loc, own_s, ag_s, ag_r, rs_s, rs_r, st_s, st_r, q_s, q_r, ex_s, ex_r, br_s, br_r, ready,
 ):
     sec = lax.axis_index("section")
     me = lax.axis_index("dev")
@@ -96,12 +96,7 @@
     ahead = [(right, left), (down, up)]
     spot = [x_, z]
 
-    greeted = [(sec, lax.rem(me + k, N_DEV)) for k in range(1, N_DEV)]
-    for s in (after, before):
-        greeted.append((s, me))
-        for k in range(1, SIDE):
-            greeted.append((s, z * SIDE + around(x_, k)))
-            greeted.append((s, around(z, k) * SIDE + x_))
+    greeted = [right, left, down, up, (after, me), (before, me)]
     barrier = pltpu.get_barrier_semaphore()
     for target in greeted:
         pl.semaphore_signal(barrier, inc=1, device_id=target, device_id_type=MESH)
@@ -331,13 +326,14 @@
             block[...] = (block[...].astype(F32) + z1[half, span].astype(F32)).astype(BF16)
         rs(half, p.at[c, around(d, 1)], z2.at[half, 0], 6, ahead[1 - half][0])
         rs(half, p.at[c, around(d, -1)], z2.at[half, 1], 7, ahead[1 - half][1])
-    passages(0)
 
     for k in (6, 7, 8):
         loads[k].wait()
     for half in range(2):
         for k in range(SIDE):
             ag_wait(half, chunk(half, (0, -1, 1, 2)[k], 2), 5 + 3 * k)
+    pl.semaphore_signal(ready, inc=1, device_id=(before, me), device_id_type=MESH)
+    passages(0)
 
     def project_queries(k):
         span = pl.ds(pl.multiple_of(k * 2 * QLEN, 2 * QLEN), 2 * QLEN)
@@ -599,6 +595,7 @@
     for g in range(1, GROUPS):
         stored(1, g)
     finish(1)
+    pl.semaphore_wait(ready, 1)
     third(0)
     join(2)
     first((2,))
@@ -703,6 +700,7 @@
             dma((2 + BLOCKS,)),
             dma((2 * BLOCKS,)),
             dma((10 * BLOCKS,)),
+            pltpu.SemaphoreType.REGULAR,
         ],
         compiler_params=pltpu.CompilerParams(
             collective_id=0, has_side_effects=True, vmem_limit_bytes=63 * 2**20

time: 197 us -> 196 us (level)
  Pallas kernels: 193 us -> 191 us
where the time goes in v5:
time: 196 us; the launch traced here: 193 us
  Pallas kernels  191 us (97%)
  other arithmetic  2.08 us (1%)
    pallas_call x1, Pallas kernels, layer(): pl.pallas_call(layer_kernel, out_shape=jax.ShapeDtypeStruct((REQ_SECTION...  191 us

profile of v5, /device:TPU:15, one launch (start us, length us, event | category | flops | bytes accessed | tf_op | source)
XLA Modules:
  0.0 192.9 jit_solution(2239314344583717336)
XLA Ops:
  0.0 190.8 %layer.1 = f32[512,512]{1,0:T(8,128)} custom-call(s32[1,64]{1,0:T(1,128)} %home.1, s32[1,2,8]{2,1,0:T(2,128)} %retrieved.1, s32[1,2,8]{2,1,0:T(2,128)} %order.1, bf16[512,512]{1,0:T(8,128)(2,1)} %bitcast.17, bf16[1232,512]{1,0:T(8,128)(2,1)} %bitcast.16, bf16[512,2048]{1,0:T(8,128)(2,1)} %bitcast.15, bf16[8192,256]{1,0:T(8,128)(2,1)} %bitcast.13, ...), custom_call_target="tpu_custom_call" | custom-call | tf_op jit(solution)/shard_map/layer/pallas_call | solution.py:645
  190.8 2.1 %convert_bitcast_fusion = bf16[1,512,512]{2,1,0:T(8,128)(2,1)} fusion(f32[512,512]{1,0:T(8,128)} %layer.1), kind=kLoop, calls=%fused_computation | loop fusion | flops 262144 | bytes 1572864 | tf_op jit(solution)/shard_map/broadcast_in_dim | solution.py:724

commit v6 on v5

--- a/solution.py
+++ b/solution.py
@@ -318,6 +318,38 @@
         far = around(spot[1 - half], 2)
         rs(half, p.at[c, far, upper], z1.at[half, upper], 4, ahead[1 - half][0])
         rs(half, p.at[c, far, lower], z1.at[half, lower], 5, ahead[1 - half][1])
+
+    for k in (6, 7, 8):
+        loads[k].wait()
+    for half in range(2):
+        for k in range(SIDE):
+            ag_wait(half, chunk(half, (0, -1, 1, 2)[k], 2), 5 + 3 * k)
+    pl.semaphore_signal(ready, inc=1, device_id=(before, me), device_id_type=MESH)
+    passages(0)
+
+    def project_queries(k):
+        span = pl.ds(pl.multiple_of(k * 2 * QLEN, 2 * QLEN), 2 * QLEN)
+        weight = qv[span, :]
+        for half in range(2):
+            qacc[half] += jnp.dot(xall[half, k], weight, preferred_element_type=F32)
+
+    qacc[...] = jnp.zeros_like(qacc)
+    loop(N_DEV, project_queries)
+    token_at = lax.broadcasted_iota(jnp.int32, (QLEN, 1), 0) + TOPK * PASS_LEN
+    token_angles = token_at.astype(F32) * frequency
+    cosine, sine = lane_tables(token_angles)
+    base = 2 * mine
+    for half in range(2):
+        for j in range(2):
+            head = turned(qacc[half, :, j * HD : (j + 1) * HD], cosine, sine)
+            q4[half, base + j] = head.astype(BF16)
+
+    def share_queries(r):
+        block = q4.at[r, pl.ds(base, 2)]
+        push(sends, block, block, q_s.at[r], q_r.at[r], pair)
+
+    share_queries(0)
+
     for half in range(2):
         p, c, d = parts[half], spot[half], spot[1 - half]
         for k, span in ((1, upper), (-1, lower)):
@@ -326,38 +358,6 @@
             block[...] = (block[...].astype(F32) + z1[half, span].astype(F32)).astype(BF16)
         rs(half, p.at[c, around(d, 1)], z2.at[half, 0], 6, ahead[1 - half][0])
         rs(half, p.at[c, around(d, -1)], z2.at[half, 1], 7, ahead[1 - half][1])
-
-    for k in (6, 7, 8):
-        loads[k].wait()
-    for half in range(2):
-        for k in range(SIDE):
-            ag_wait(half, chunk(half, (0, -1, 1, 2)[k], 2), 5 + 3 * k)
-    pl.semaphore_signal(ready, inc=1, device_id=(before, me), device_id_type=MESH)
-    passages(0)
-
-    def project_queries(k):
-        span = pl.ds(pl.multiple_of(k * 2 * QLEN, 2 * QLEN), 2 * QLEN)
-        weight = qv[span, :]
-        for half in range(2):
-            qacc[half] += jnp.dot(xall[half, k], weight, preferred_element_type=F32)
-
-    qacc[...] = jnp.zeros_like(qacc)
-    loop(N_DEV, project_queries)
-    token_at = lax.broadcasted_iota(jnp.int32, (QLEN, 1), 0) + TOPK * PASS_LEN
-    token_angles = token_at.astype(F32) * frequency
-    cosine, sine = lane_tables(token_angles)
-    base = 2 * mine
-    for half in range(2):
-        for j in range(2):
-            head = turned(qacc[half, :, j * HD : (j + 1) * HD], cosine, sine)
-            q4[half, base + j] = head.astype(BF16)
-
-    def share_queries(r):
-        block = q4.at[r, pl.ds(base, 2)]
-        push(sends, block, block, q_s.at[r], q_r.at[r], pair)
-
-    share_queries(0)
-
     for g in range(1, GROUPS):
         passages(g)
     share_queries(1)

time: 196 us -> 196 us (level)
  no operation moved by 1% of the time
where the time goes in v6:
time: 196 us; the launch traced here: 193 us
  Pallas kernels  190 us (97%)
  other arithmetic  2.08 us (1%)
    pallas_call x1, Pallas kernels, layer(): pl.pallas_call(layer_kernel, out_shape=jax.ShapeDtypeStruct((REQ_SECTION...  190 us

profile of v6, /device:TPU:15, one launch (start us, length us, event | category | flops | bytes accessed | tf_op | source)
XLA Modules:
  0.0 192.6 jit_solution(16944438711133111129)
XLA Ops:
  0.0 190.5 %layer.1 = f32[512,512]{1,0:T(8,128)} custom-call(s32[1,64]{1,0:T(1,128)} %home.1, s32[1,2,8]{2,1,0:T(2,128)} %retrieved.1, s32[1,2,8]{2,1,0:T(2,128)} %order.1, bf16[512,512]{1,0:T(8,128)(2,1)} %bitcast.17, bf16[1232,512]{1,0:T(8,128)(2,1)} %bitcast.16, bf16[512,2048]{1,0:T(8,128)(2,1)} %bitcast.15, bf16[8192,256]{1,0:T(8,128)(2,1)} %bitcast.13, ...), custom_call_target="tpu_custom_call" | custom-call | tf_op jit(solution)/shard_map/layer/pallas_call | solution.py:645
  190.5 2.1 %convert_bitcast_fusion = bf16[1,512,512]{2,1,0:T(8,128)(2,1)} fusion(f32[512,512]{1,0:T(8,128)} %layer.1), kind=kLoop, calls=%fused_computation | loop fusion | flops 262144 | bytes 1572864 | tf_op jit(solution)/shard_map/broadcast_in_dim | solution.py:724
